TPU v7x, 256 devices: a whole 4x4x8 slice. The times are simulated.
256 devices in a mesh: section: 2 (over x_hi), cfg: 2 (over core), req: 4 (over y), sp: 16 (over x_lo, z).
Axes of the slice: x: 4 (x_hi: 2, x_lo: 2; x = x_hi * 2 + x_lo), y: 4, z: 8, core: 2. Of those that a mesh axis runs over, the one named last changes fastest.
Arguments:
- qkv: bfloat16 [2, 2, 10240, 3, 32, 128], P('section', 'cfg', ('req', 'sp')), parts along dimension 2, may hold values from -6 to 6
- counts: int32 [2, 4], P('section', 'req'), parts along dimension 1, may hold values from 1920 to 2560, as said below
- timesteps: int32 [2, 4], P('section', 'req'), parts along dimension 1, may hold values from 0 to 999
- block_map: int32 [10240], P(('req', 'sp')), parts along dimension 0, may hold values from 0 to 2559
- w_out: bfloat16 [32, 128, 64], replicated, may hold values from -0.09375 to 0.09375
- w_in: bfloat16 [64, 32, 128], replicated, may hold values from -0.75 to 0.75
Outputs:
- result: bfloat16 [2, 10240, 2, 16, 128], P('section', ('req', 'sp'), 'cfg'), parts along dimension 1
There are 4 independent parts, one for each index of `req`. A program takes and returns all parts, laid end to end along the dimension named above; an argument that names none is the same for every part. Nothing has to cross between parts.
Inputs may be any that keep to these rules, and one draw needn't show every extreme that they name: `counts`: at least 1920 in both sections, and exactly 2560 in one of them.
All inputs are finite; a program needn't handle non-finite values.
Results may differ from a plain program's by a relative error of at most 0.008.
Values may be sent and summed in bfloat16 or wider, within the bound.
A program may use at most 64 MiB of HBM per device.

v0:
```python
import math

import jax
import jax.numpy as jnp
from jax import lax
from jax.sharding import PartitionSpec as P


def passed_along(value, axis, steps):
    count = lax.axis_size(axis)
    initial, last = (max(0, -steps), min(count, count - steps))
    return lax.ppermute(value, axis, [(source, source + steps) for source in range(initial, last)])


def gate_rows(tstep, head_ids, head_size):
    dims = jnp.arange(head_size).astype(jnp.float32)
    freq = jnp.exp(-math.log(10000.0) * dims / head_size)
    return 1.0 + 0.5 * jnp.sin(
        tstep.astype(jnp.float32) * freq[None, :] + 0.7 * head_ids.astype(jnp.float32)[:, None]
    )


def on_device(qkv, counts, timesteps, block_map, w_out, w_in):
    n_sp = lax.axis_size("sp")
    tok_dev = qkv.shape[2]
    heads = qkv.shape[4]
    head_size = qkv.shape[5]
    seq = tok_dev * n_sp
    local_heads = heads // n_sp
    sp_idx = lax.axis_index("sp")
    cfg_idx = lax.axis_index("cfg")
    count = counts[0, 0]
    tstep = timesteps[0, 0]
    latent_width = w_out.shape[2]
    grouped = qkv[0, 0].reshape(tok_dev, 3, n_sp, local_heads, head_size)
    block = math.gcd(seq, 512)
    keys_ok = jnp.arange(seq) < count
    piece = lax.all_to_all(grouped, "sp", split_axis=2, concat_axis=0, tiled=True)
    query = piece[:, 0, 0]
    keys = piece[:, 1, 0]
    values = piece[:, 2, 0]
    width = query.shape[1]
    query_blocks = query.reshape(seq // block, block, width, head_size)

    def one_block(query_block):
        scores = jnp.einsum(
            "qhd,khd->hqk", query_block, keys, preferred_element_type=jnp.float32
        ) * head_size ** (-0.5)
        scores = jnp.where(keys_ok[None, None, :], scores, -1e30)
        top = jnp.max(scores, axis=-1, keepdims=True)
        expo = jnp.where(keys_ok[None, None, :], jnp.exp(scores - top), 0.0)
        total = jnp.sum(expo, axis=-1)
        mixed = jnp.einsum(
            "hqk,khd->qhd", expo.astype(jnp.bfloat16), values, preferred_element_type=jnp.float32
        )
        return (mixed / jnp.transpose(total)[:, :, None]).astype(jnp.bfloat16)

    mixed_all = lax.map(one_block, query_blocks).reshape(seq, width, head_size)
    attended = mixed_all[:, None]
    returned = lax.all_to_all(attended, "sp", split_axis=0, concat_axis=1, tiled=True)
    split = returned.reshape(1, tok_dev, heads // 2, 2, head_size)
    both = lax.all_to_all(split, "cfg", split_axis=3, concat_axis=0, tiled=True)
    cond = both[0, :, :, 0].astype(jnp.float32)
    uncond = both[1, :, :, 0].astype(jnp.float32)
    head_ids = 2 * jnp.arange(heads // 2) + cfg_idx
    positions = sp_idx * tok_dev + jnp.arange(tok_dev)
    valid = (positions < count).astype(jnp.float32)
    guided = uncond + 5.0 * (cond - uncond)
    gate = gate_rows(tstep, head_ids, head_size)
    branch = (gate[None] * guided * valid[:, None, None]).astype(jnp.bfloat16)
    out_rows = lax.dynamic_index_in_dim(
        w_out.reshape(heads // 2, 2, head_size, latent_width), cfg_idx, 1, keepdims=False
    )
    partial_latent = jnp.dot(
        branch.reshape(tok_dev, -1),
        out_rows.reshape(-1, latent_width),
        preferred_element_type=jnp.float32,
    )
    latent = lax.psum(partial_latent, "cfg").astype(jnp.bfloat16)
    collected = lax.all_gather(latent, "sp", axis=0, tiled=True)
    handed = passed_along(collected, "section", 1)
    picked = jnp.take(handed, block_map, axis=0)
    in_cols = lax.dynamic_index_in_dim(
        w_in.reshape(latent_width, heads // 2, 2, head_size), cfg_idx, 2, keepdims=False
    )
    lifted = jnp.dot(picked, in_cols.reshape(latent_width, -1), preferred_element_type=jnp.float32)
    result = (branch.reshape(tok_dev, -1).astype(jnp.float32) + lifted).astype(jnp.bfloat16)
    return result.reshape(1, tok_dev, 1, heads // 2, head_size)


def solution(mesh):
    placed = (
        P("section", "cfg", ("req", "sp"), None, None, None),
        P("section", "req"),
        P("section", "req"),
        P(("req", "sp")),
        P(),
        P(),
    )
    return jax.shard_map(
        on_device,
        mesh=mesh,
        in_specs=placed,
        out_specs=P("section", ("req", "sp"), "cfg", None, None),
        check_vma=False,
    )
```

profile of v0, /device:TPU:20, one launch (start us, length us, event | category | flops | bytes accessed | tf_op | source)
XLA Modules:
  0.0 284.6 jit_solution(6451190047291705591)
XLA Ops:
  0.0 5.6 %copy.45 = bf16[160,3,16,2,128]{4,0,3,1,2:T(8,128)(2,1)} copy(bf16[160,3,16,2,128]{4,3,2,1,0:T(2,128)(2,1)} %bitcast.141) | data formatting | bytes 7864320 | tf_op jit(solution)/shard_map/reshape;squeeze | solution.py:35
  5.6 9.2 %all-to-all-start = ((bf16[160,3,16,2,128]{4,0,3,1,2:T(8,128)(2,1)}), bf16[160,3,16,2,128]{4,0,3,1,2:T(8,128)(2,1)}, u32[]{:S(2)}, u32[]{:S(2)}) async-start(bf16[160,3,16,2,128]{4,0,3,1,2:T(8,128)(2,1)} %copy.45), calls=%async_computation | async-start | bytes 7864320 | tf_op jit(solution)/shard_map/all_to_all | solution.py:38
  14.9 89.6 %all-to-all-done = bf16[160,3,16,2,128]{4,0,3,1,2:T(8,128)(2,1)} async-done(((bf16[160,3,16,2,128]{4,0,3,1,2:T(8,128)(2,1)}), bf16[160,3,16,2,128]{4,0,3,1,2:T(8,128)(2,1)}, u32[]{:S(2)}, u32[]{:S(2)}) %all-to-all-start) | async-done | bytes 3932192 | tf_op jit(solution)/shard_map/all_to_all | solution.py:38
  104.4 2.5 copy.46
  106.9 1.8 slice_bitcast_fusion
  108.7 62.3 %while.11 = (s32[]{:T(128)}, bf16[5,512,2,128]{3,1,0,2:T(8,128)(2,1)S(1)}, bf16[5,512,2,128]{3,1,0,2:T(8,128)(2,1)}, bf16[2560,2,128]{2,0,1:T(8,128)(2,1)}, bf16...) while((s32[]{:T(128)}, bf16[5,512,2,128]{3,1,0,2:T(8,128)(2,1)S(1)}, ...), condition=%wide.region_3.4_spmd.clone, body=%wide.region_0.3_spmd.clone.sunk | while | flops 1358173184 | bytes 13648981 | solution.py:58
  109.3 7.7 %fusion.77 = (f32[2,512]{1,0:T(2,128)S(1)}, bf16[2,512,2560]{2,1,0:T(8,128)(2,1)}) fusion(pred[2560]{0:T(1024)(128)(4,1)S(1)} %iota_compare_fusion.2, bf16[2560,2,128]{2,0,1:T(8,128)(2,1)} %get-tuple-element.156, bf16[5,512,2,128]{3,1,0,2:T(8,128)(2,1)} %get-tuple-element.155, s32[]{:T(128)} %get-tuple-element.146), kind=kOutput, calls=%fused_computation.66.clone.1 | convolution fusion | flops 686819840 | bytes 6826496 | tf_op jit(solution)/shard_map/while/body/eval_jaxpr/sub | solution.py:51
  117.1 4.0 %fusion.78 = bf16[5,512,2,128]{3,1,0,2:T(8,128)(2,1)S(1)} fusion(bf16[5,512,2,128]{3,1,0,2:T(8,128)(2,1)S(1)} %get-tuple-element.147, s32[]{:T(128)} %get-tuple-element.146, bf16[2560,2,128]{2,0,1:T(8,128)(2,1)S(1)} %get-tuple-element.157, bf16[2,512,2560]{2,1,0:T(8,128)(2,1)} %get-tuple-element.137, f32[512,2]{0,1:T(2,128)S(1)} %bitcast.150), kind=kOutput, calls=%fused_computation.16.clone.1 | convolution fusion | flops 671350784 | bytes 6819844 | tf_op jit(solution)/shard_map/while/body/eval_jaxpr/hqk,khd->qhd/dot_general | solution.py:53
  121.8 7.7 %fusion.77 = (f32[2,512]{1,0:T(2,128)S(1)}, bf16[2,512,2560]{2,1,0:T(8,128)(2,1)}) fusion(pred[2560]{0:T(1024)(128)(4,1)S(1)} %iota_compare_fusion.2, bf16[2560,2,128]{2,0,1:T(8,128)(2,1)} %get-tuple-element.156, bf16[5,512,2,128]{3,1,0,2:T(8,128)(2,1)} %get-tuple-element.155, s32[]{:T(128)} %get-tuple-element.146), kind=kOutput, calls=%fused_computation.66.clone.1 | convolution fusion | flops 686819840 | bytes 6826496 | tf_op jit(solution)/shard_map/while/body/eval_jaxpr/sub | solution.py:51
  129.5 4.0 %fusion.78 = bf16[5,512,2,128]{3,1,0,2:T(8,128)(2,1)S(1)} fusion(bf16[5,512,2,128]{3,1,0,2:T(8,128)(2,1)S(1)} %get-tuple-element.147, s32[]{:T(128)} %get-tuple-element.146, bf16[2560,2,128]{2,0,1:T(8,128)(2,1)S(1)} %get-tuple-element.157, bf16[2,512,2560]{2,1,0:T(8,128)(2,1)} %get-tuple-element.137, f32[512,2]{0,1:T(2,128)S(1)} %bitcast.150), kind=kOutput, calls=%fused_computation.16.clone.1 | convolution fusion | flops 671350784 | bytes 6819844 | tf_op jit(solution)/shard_map/while/body/eval_jaxpr/hqk,khd->qhd/dot_general | solution.py:53
  134.3 7.7 %fusion.77 = (f32[2,512]{1,0:T(2,128)S(1)}, bf16[2,512,2560]{2,1,0:T(8,128)(2,1)}) fusion(pred[2560]{0:T(1024)(128)(4,1)S(1)} %iota_compare_fusion.2, bf16[2560,2,128]{2,0,1:T(8,128)(2,1)} %get-tuple-element.156, bf16[5,512,2,128]{3,1,0,2:T(8,128)(2,1)} %get-tuple-element.155, s32[]{:T(128)} %get-tuple-element.146), kind=kOutput, calls=%fused_computation.66.clone.1 | convolution fusion | flops 686819840 | bytes 6826496 | tf_op jit(solution)/shard_map/while/body/eval_jaxpr/sub | solution.py:51
  142.0 4.0 %fusion.78 = bf16[5,512,2,128]{3,1,0,2:T(8,128)(2,1)S(1)} fusion(bf16[5,512,2,128]{3,1,0,2:T(8,128)(2,1)S(1)} %get-tuple-element.147, s32[]{:T(128)} %get-tuple-element.146, bf16[2560,2,128]{2,0,1:T(8,128)(2,1)S(1)} %get-tuple-element.157, bf16[2,512,2560]{2,1,0:T(8,128)(2,1)} %get-tuple-element.137, f32[512,2]{0,1:T(2,128)S(1)} %bitcast.150), kind=kOutput, calls=%fused_computation.16.clone.1 | convolution fusion | flops 671350784 | bytes 6819844 | tf_op jit(solution)/shard_map/while/body/eval_jaxpr/hqk,khd->qhd/dot_general | solution.py:53
  146.7 7.7 %fusion.77 = (f32[2,512]{1,0:T(2,128)S(1)}, bf16[2,512,2560]{2,1,0:T(8,128)(2,1)}) fusion(pred[2560]{0:T(1024)(128)(4,1)S(1)} %iota_compare_fusion.2, bf16[2560,2,128]{2,0,1:T(8,128)(2,1)} %get-tuple-element.156, bf16[5,512,2,128]{3,1,0,2:T(8,128)(2,1)} %get-tuple-element.155, s32[]{:T(128)} %get-tuple-element.146), kind=kOutput, calls=%fused_computation.66.clone.1 | convolution fusion | flops 686819840 | bytes 6826496 | tf_op jit(solution)/shard_map/while/body/eval_jaxpr/sub | solution.py:51
  154.4 4.0 %fusion.78 = bf16[5,512,2,128]{3,1,0,2:T(8,128)(2,1)S(1)} fusion(bf16[5,512,2,128]{3,1,0,2:T(8,128)(2,1)S(1)} %get-tuple-element.147, s32[]{:T(128)} %get-tuple-element.146, bf16[2560,2,128]{2,0,1:T(8,128)(2,1)S(1)} %get-tuple-element.157, bf16[2,512,2560]{2,1,0:T(8,128)(2,1)} %get-tuple-element.137, f32[512,2]{0,1:T(2,128)S(1)} %bitcast.150), kind=kOutput, calls=%fused_computation.16.clone.1 | convolution fusion | flops 671350784 | bytes 6819844 | tf_op jit(solution)/shard_map/while/body/eval_jaxpr/hqk,khd->qhd/dot_general | solution.py:53
  159.2 7.7 %fusion.77 = (f32[2,512]{1,0:T(2,128)S(1)}, bf16[2,512,2560]{2,1,0:T(8,128)(2,1)}) fusion(pred[2560]{0:T(1024)(128)(4,1)S(1)} %iota_compare_fusion.2, bf16[2560,2,128]{2,0,1:T(8,128)(2,1)} %get-tuple-element.156, bf16[5,512,2,128]{3,1,0,2:T(8,128)(2,1)} %get-tuple-element.155, s32[]{:T(128)} %get-tuple-element.146), kind=kOutput, calls=%fused_computation.66.clone.1 | convolution fusion | flops 686819840 | bytes 6826496 | tf_op jit(solution)/shard_map/while/body/eval_jaxpr/sub | solution.py:51
  166.9 4.0 %fusion.78 = bf16[5,512,2,128]{3,1,0,2:T(8,128)(2,1)S(1)} fusion(bf16[5,512,2,128]{3,1,0,2:T(8,128)(2,1)S(1)} %get-tuple-element.147, s32[]{:T(128)} %get-tuple-element.146, bf16[2560,2,128]{2,0,1:T(8,128)(2,1)S(1)} %get-tuple-element.157, bf16[2,512,2560]{2,1,0:T(8,128)(2,1)} %get-tuple-element.137, f32[512,2]{0,1:T(2,128)S(1)} %bitcast.150), kind=kOutput, calls=%fused_computation.16.clone.1 | convolution fusion | flops 671350784 | bytes 6819844 | tf_op jit(solution)/shard_map/while/body/eval_jaxpr/hqk,khd->qhd/dot_general | solution.py:53
  171.0 11.6 %copy.49 = bf16[2560,1,2,128]{3,2,1,0:T(2,128)(2,1)} copy(bf16[2560,1,2,128]{3,0,2,1:T(8,128)(2,1)S(1)} %bitcast.142) | data formatting | bytes 2621440 | tf_op jit(solution)/shard_map/broadcast_in_dim;reshape | solution.py:59
  182.6 6.8 %all-to-all-start.1 = ((bf16[2560,1,2,128]{3,2,1,0:T(2,128)(2,1)}), bf16[2560,1,2,128]{3,2,1,0:T(2,128)(2,1)S(1)}, u32[]{:S(2)}, u32[]{:S(2)}) async-start(bf16[2560,1,2,128]{3,2,1,0:T(2,128)(2,1)} %copy.49), calls=%async_computation.1 | async-start | bytes 2621440 | tf_op jit(solution)/shard_map/all_to_all | solution.py:60
  191.3 30.6 %all-to-all-done.1 = bf16[2560,1,2,128]{3,2,1,0:T(2,128)(2,1)S(1)} async-done(((bf16[2560,1,2,128]{3,2,1,0:T(2,128)(2,1)}), bf16[2560,1,2,128]{3,2,1,0:T(2,128)(2,1)S(1)}, u32[]{:S(2)}, u32[]{:S(2)}) %all-to-all-start.1) | async-done | bytes 1310752 | tf_op jit(solution)/shard_map/all_to_all | solution.py:60
  222.1 4.8 %all_to_all.48 = bf16[1,160,16,2,128]{4,1,2,0,3:T(8,128)(2,1)S(1)} all-to-all(bf16[1,160,16,2,128]{4,1,2,0,3:T(8,128)(2,1)S(1)} %bitcast.140), channel_id=1, replica_groups=mesh['section'=2,'cfg'=2,'req'=4,'sp'=16] {'cfg'}, dimensions={3} | all-to-all | bytes 2621440 | tf_op jit(solution)/shard_map/all_to_all | solution.py:62
  227.8 3.7 %psum.7 = bf16[160,64]{0,1:T(8,128)(2,1)S(1)} all-reduce(f32[160,64]{0,1:T(8,128)S(1)} %fusion.47), channel_id=1, replica_groups=mesh['section'=2,'cfg'=2,'req'=4,'sp'=16] {'cfg'}, use_global_device_ids=true, to_apply=%region_4.5 | all-reduce | flops 10240 | bytes 61440 | tf_op jit(solution)/shard_map/psum | solution.py:79
  231.6 34.6 %all-gather = bf16[16,160,64]{1,2,0:T(8,128)(2,1)S(1)} all-gather(bf16[1,160,64]{1,2,0:T(8,128)(2,1)S(1)} %bitcast.148), channel_id=1, replica_groups=mesh['section'=2,'cfg'=2,'req'=4,'sp'=16] {'sp'}, dimensions={0}, use_global_device_ids=true | all-gather | bytes 348160 | tf_op jit(solution)/shard_map/all_gather | solution.py:80
  266.5 1.5 reshape.132
  267.9 1.3 collective-permute-start
  269.2 1.5 dynamic-slice_reduce_fusion
  271.1 0.8 copy.52
  271.8 0.8 copy.53
  272.6 6.1 %collective-permute-done = bf16[2560,64]{0,1:T(8,128)(2,1)} collective-permute-done((bf16[2560,64]{0,1:T(8,128)(2,1)}, bf16[2560,64]{0,1:T(8,128)(2,1)}, u32[]{:S(2)}, u32[]{:S(2)}) %collective-permute-start) | collective-permute-done | bytes 327712 | tf_op jit(solution)/shard_map/ppermute | solution.py:12
  278.7 2.1 copy.57
  280.8 1.9 gather_fusion
  282.6 1.0 fusion.46
  283.6 1.0 copy.72
  (29 shorter events, 5.5 us)
Async XLA Ops:
  0.0 190.7 %copy-start = (bf16[32,128,64]{1,2,0:T(8,128)(2,1)S(1)}, bf16[32,128,64]{1,2,0:T(8,128)(2,1)}, u32[]{:S(2)}) copy-start(bf16[32,128,64]{1,2,0:T(8,128)(2,1)} %param.12) | copy-start | bytes 1572868
  5.6 98.8 %all-to-all-start = ((bf16[160,3,16,2,128]{4,0,3,1,2:T(8,128)(2,1)}), bf16[160,3,16,2,128]{4,0,3,1,2:T(8,128)(2,1)}, u32[]{:S(2)}, u32[]{:S(2)}) async-start(bf16[160,3,16,2,128]{4,0,3,1,2:T(8,128)(2,1)} %copy.45), calls=%async_computation | async-start | bytes 7864320 | tf_op jit(solution)/shard_map/all_to_all | solution.py:38
  182.6 8.4 %copy-start.2 = (s32[160]{0:T(256)S(1)}, s32[160]{0:T(256)}, u32[]{:S(2)}) copy-start(s32[160]{0:T(256)} %param.11) | copy-start | bytes 1924
  182.6 39.3 %all-to-all-start.1 = ((bf16[2560,1,2,128]{3,2,1,0:T(2,128)(2,1)}), bf16[2560,1,2,128]{3,2,1,0:T(2,128)(2,1)S(1)}, u32[]{:S(2)}, u32[]{:S(2)}) async-start(bf16[2560,1,2,128]{3,2,1,0:T(2,128)(2,1)} %copy.49), calls=%async_computation.1 | async-start | bytes 2621440 | tf_op jit(solution)/shard_map/all_to_all | solution.py:60
  227.8 41.4 %copy-start.1 = (bf16[64,32,128]{2,1,0:T(8,128)(2,1)S(1)}, bf16[64,32,128]{2,1,0:T(8,128)(2,1)}, u32[]{:S(2)}) copy-start(bf16[64,32,128]{2,1,0:T(8,128)(2,1)} %param.13) | copy-start | bytes 1572868
  267.9 10.8 %collective-permute-start = (bf16[2560,64]{0,1:T(8,128)(2,1)}, bf16[2560,64]{0,1:T(8,128)(2,1)}, u32[]{:S(2)}, u32[]{:S(2)}) collective-permute-start(bf16[2560,64]{0,1:T(8,128)(2,1)} %reshape.132), channel_id=1, source_target_pairs={{0,128},{1,129},{2,130},{3,131},{4,132},{5,133},{6,134},{7,135},{8... | collective-permute-start | bytes 983048 | tf_op jit(solution)/shard_map/ppermute | solution.py:12
where the time goes:
time: 285 us
  waiting for transfers between devices  126 us (44%)
  matrix products  60.3 us (21%)
  blocking collectives  43.1 us (15%)
  local copies, waits for them, and re-layouts  31.9 us (11%)
  starting transfers between devices  17.3 us (6%)
  other arithmetic  4.13 us (1%)
    all_to_all x1, waiting for transfers between devices, on_device(): lax.all_to_all(grouped, 'sp', split_axis=2, concat_axis=0, tiled=True)  89.6 us
    sub x5, matrix products, one_block(): expo = jnp.where(keys_ok[None, None, :], jnp.exp(scores - top), 0.0)  38.7 us
    all_gather x1, blocking collectives, on_device(): collected = lax.all_gather(latent, 'sp', axis=0, tiled=True)  34.6 us
    all_to_all x1, waiting for transfers between devices, on_device(): lax.all_to_all(attended, 'sp', split_axis=0, concat_axis=1, tiled=True)  30.6 us
    dot_general x5, matrix products, one_block(): jnp.einsum('hqk,khd->qhd', expo.astype(jnp.bfloat16), values, preferred_e...  20.2 us
    another operation x1, local copies, waits for them, and re-layouts, on_device(): attended = mixed_all[:, None]  11.6 us
    all_to_all x1, starting transfers between devices, on_device(): lax.all_to_all(grouped, 'sp', split_axis=2, concat_axis=0, tiled=True)  9.25 us
    all_to_all x1, starting transfers between devices, on_device(): lax.all_to_all(attended, 'sp', split_axis=0, concat_axis=1, tiled=True)  6.82 us
  transfers between devices with their start and end apart: 3, of which 3 were waited for; matrix products, arithmetic and copies ran while one was open for 1% of the time, Pallas kernels for 0%

commit v1 on v0

v1 whole, which is shorter than its diff:
```python
import math

import jax
import jax.numpy as jnp
from jax import lax
from jax.experimental import pallas as pl
from jax.experimental.pallas import tpu as pltpu
from jax.sharding import PartitionSpec as P

MESH = pl.DeviceIdType.MESH
F32 = jnp.float32
BF16 = jnp.bfloat16


def kernel(
    n_sp, tok, heads, hd, width,
    qkv_ref, cnt_ref, ts_ref, bm_ref, wo_ref, wi_ref, out_ref,
    xin, stage, qland, kland, vaug, kt, sc, att_mine, att_send, att_recv, brs, brl,
    lat_mine, lat_recv, psum_send, psum_recv, onehot, wo, wi, w2, gate,
    in_sem, w_sem, own_sem, s_sem, r_sem, sib_s, sib_r, br_s, br_r, ps_s, ps_r, lat_s, lat_r,
):
    seq = tok * n_sp
    half = tok // 2
    n_z = n_sp // 2
    sec = lax.axis_index("section")
    core = lax.axis_index("cfg")
    me = lax.axis_index("sp")
    count = cnt_ref[0, 0]
    scale = hd ** -0.5 * math.log2(math.e)

    def offset(step):
        turn = step // 2
        dz = ((turn + 1) // 2) * (1 - 2 * ((turn + 1) % 2))
        return step % 2, dz

    def to_peer(step):
        dx, dz = offset(step)
        return ((me // n_z + dx) % 2) * n_z + (me % n_z + dz + n_z) % n_z

    def from_peer(step):
        dx, dz = offset(step)
        return ((me // n_z + dx) % 2) * n_z + (me % n_z - dz + n_z) % n_z

    loads = [
        pltpu.make_async_copy(qkv_ref.at[:, c], xin.at[c], in_sem.at[c]) for c in (0, 1, 2)
    ]
    for c in (1, 2, 0):
        loads[c].start()
    load_wo = pltpu.make_async_copy(wo_ref, wo, w_sem.at[0])
    load_wi = pltpu.make_async_copy(wi_ref, wi, w_sem.at[1])
    load_wo.start()
    load_wi.start()

    barrier = pltpu.get_barrier_semaphore()

    def greet(step, carry):
        peer = to_peer(step)
        pl.semaphore_signal(barrier, inc=1, device_id={"sp": peer}, device_id_type=MESH)
        pl.semaphore_signal(
            barrier, inc=1, device_id={"section": 1 - sec, "sp": peer}, device_id_type=MESH
        )
        return carry

    lax.fori_loop(1, n_sp, greet, 0)
    pl.semaphore_signal(barrier, inc=1, device_id={"cfg": 1 - core}, device_id_type=MESH)
    pl.semaphore_signal(barrier, inc=1, device_id={"section": 1 - sec}, device_id_type=MESH)

    def transpose_kind(c):
        def body(t, carry):
            rows = pl.ds(pl.multiple_of(t * 16, 16), 16)
            stage[c, :, rows, :] = jnp.swapaxes(xin[c, rows], 0, 1)
            return carry

        lax.fori_loop(0, tok // 16, body, 0)

    def landing(c, source):
        if c == 0:
            return qland.at[source]
        rows = pl.ds(pl.multiple_of(source * tok, tok), tok)
        if c == 1:
            return kland.at[:, rows, :]
        return vaug.at[:, rows, pl.ds(0, hd)]

    def qkv_copy(c, target):
        return pltpu.make_async_remote_copy(
            src_ref=stage.at[c, pl.ds(2 * target, 2)],
            dst_ref=landing(c, me),
            send_sem=s_sem.at[c, target],
            recv_sem=r_sem.at[c, me],
            device_id={"sp": target},
            device_id_type=MESH,
        )

    def qkv_arrival(c, source):
        return pltpu.make_async_remote_copy(
            src_ref=stage.at[c, pl.ds(2 * source, 2)],
            dst_ref=landing(c, source),
            send_sem=s_sem.at[c, source],
            recv_sem=r_sem.at[c, source],
            device_id={"sp": source},
            device_id_type=MESH,
        )

    def own_copy(c):
        return pltpu.make_async_copy(
            stage.at[c, pl.ds(2 * me, 2)], landing(c, me), own_sem.at[c]
        )

    def send_kind(c):
        def body(step, carry):
            qkv_copy(c, to_peer(step)).start()
            return carry

        lax.fori_loop(1, n_sp, body, 0)
        own_copy(c).start()

    loads[1].wait()
    transpose_kind(1)
    pl.semaphore_wait(barrier, 2 * n_sp)
    send_kind(1)
    loads[2].wait()
    transpose_kind(2)
    send_kind(2)
    loads[0].wait()
    transpose_kind(0)
    send_kind(0)

    head_id = (2 * me + core).astype(F32)
    dims = lax.broadcasted_iota(jnp.int32, (8, hd), 1).astype(F32)
    freq = jnp.exp(-math.log(10000.0) * dims / hd)
    gate[...] = 1.0 + 0.5 * jnp.sin(ts_ref[0, 0].astype(F32) * freq + 0.7 * head_id)

    key_rows = lax.broadcasted_iota(jnp.int32, (seq, hd), 0)
    ones = jnp.where(key_rows < count, 1.0, 0.0).astype(BF16)
    vaug[0, :, hd:] = ones
    vaug[1, :, hd:] = ones

    load_wo.wait()
    load_wi.wait()

    @pl.when(sec == 1)
    def _():
        def turn(t, carry):
            rows = pl.ds(pl.multiple_of(t * 16, 16), 16)
            stacked = jnp.swapaxes(wi[rows], 0, 1).reshape(heads // 2, 2, 16, hd)
            part = jnp.where(core == 0, stacked[:, 0], stacked[:, 1])
            w2[:, rows, :] = part
            w2[:, pl.ds(pl.multiple_of(width + t * 16, 16), 16), :] = part
            return carry

        lax.fori_loop(0, width // 16, turn, 0)
        eye = lax.broadcasted_iota(jnp.int32, (tok, tok), 0) == lax.broadcasted_iota(
            jnp.int32, (tok, tok), 1
        )
        wanted = jnp.sum(
            jnp.where(eye, jnp.broadcast_to(bm_ref[...], (tok, tok)).astype(F32), 0.0),
            axis=1, keepdims=True,
        ).astype(jnp.int32)
        owner = wanted // tok
        row = wanted - owner * tok
        upper = (row >= half).astype(jnp.int32)
        slot = owner * half + row - upper * half
        places = lax.broadcasted_iota(jnp.int32, (tok, n_sp * half), 1)
        onehot[0] = jnp.where(places == jnp.where(upper == 0, slot, -1), 1.0, 0.0).astype(BF16)
        onehot[1] = jnp.where(places == jnp.where(upper == 1, slot, -1), 1.0, 0.0).astype(BF16)

    def wait_kind(c):
        def body(step, carry):
            qkv_arrival(c, from_peer(step)).wait_recv()
            return carry

        lax.fori_loop(1, n_sp, body, 0)
        own_copy(c).wait()

    quarter = seq // 4
    tail_ok = 3 * quarter + lax.broadcasted_iota(jnp.int32, (quarter, hd), 0) < count
    wait_kind(1)
    for h in (0, 1):
        for part in range(4):
            rows = slice(part * quarter, (part + 1) * quarter)
            block = kland[h, rows].astype(F32)
            if part == 3:
                block = jnp.where(tail_ok, block, kland[h, 0:16].astype(F32)[0:1])
            kt[h, :, rows] = block.T.astype(BF16)
    wait_kind(2)
    for h in (0, 1):
        tail = vaug[h, 3 * quarter:, :hd].astype(F32)
        vaug[h, 3 * quarter:, :hd] = jnp.where(tail_ok, tail, 0.0).astype(BF16)

    def sibling_copy(source):
        return pltpu.make_async_remote_copy(
            src_ref=att_send.at[source],
            dst_ref=att_recv.at[source],
            send_sem=sib_s.at[source],
            recv_sem=sib_r.at[source],
            device_id={"cfg": 1 - core},
            device_id_type=MESH,
        )

    def branch_copy(target):
        return pltpu.make_async_remote_copy(
            src_ref=brs.at[target],
            dst_ref=brl.at[me],
            send_sem=br_s.at[target],
            recv_sem=br_r.at[me],
            device_id={"sp": target},
            device_id_type=MESH,
        )

    def branch_arrival(source):
        return pltpu.make_async_remote_copy(
            src_ref=brs.at[source],
            dst_ref=brl.at[source],
            send_sem=br_s.at[source],
            recv_sem=br_r.at[source],
            device_id={"sp": source},
            device_id_type=MESH,
        )

    def attend(step):
        source = from_peer(step)
        for h in (0, 1):
            sc[h] = jnp.dot(qland[source, h], kt[h], preferred_element_type=F32)
        done = []
        for h in (0, 1):
            top = jnp.max(sc[h], axis=1, keepdims=True) * scale
            weights = jnp.exp2(sc[h] * scale - top).astype(BF16)
            mixed = jnp.dot(weights, vaug[h], preferred_element_type=F32)
            done.append(mixed[:, :hd] / mixed[:, hd:])
        att_mine[source] = jnp.where(core == 0, done[0], done[1]).astype(BF16)
        att_send[source] = jnp.where(core == 0, done[1], done[0]).astype(BF16)
        sibling_copy(source).start()

    def combine(step):
        source = from_peer(step)
        sibling_copy(source).wait_recv()
        mine = att_mine[source].astype(F32)
        theirs = att_recv[source].astype(F32)
        cond = jnp.where(core == 0, mine, theirs)
        uncond = jnp.where(core == 0, theirs, mine)
        guided = uncond + 5.0 * (cond - uncond)
        position = source * tok + lax.broadcasted_iota(jnp.int32, (tok, hd), 0)
        return source, jnp.where(position < count, gate[0:1] * guided, 0.0).astype(BF16)

    def send_branch(step):
        target, block = combine(step)
        brs[target] = block
        branch_copy(target).start()

    own_copy(0).wait()
    attend(0)

    def first(step, carry):
        qkv_arrival(0, from_peer(step)).wait_recv()
        attend(step)

        @pl.when(step == 1)
        def _():
            source, block = combine(0)
            brl[source] = block

        @pl.when(step > 1)
        def _():
            send_branch(step - 1)

        return carry

    lax.fori_loop(1, n_sp, first, 0)
    send_branch(n_sp - 1)

    @pl.when(sec == 0)
    def _():
        def project(step, total):
            source = from_peer(step)

            @pl.when(step > 0)
            def _():
                branch_arrival(source).wait_recv()

            block = brl[source]
            out_ref[source] = block
            return total + lax.dot_general(
                block, wo[2 * source + core], (((1,), (1,)), ((), ())),
                preferred_element_type=F32,
            )

        total = lax.fori_loop(0, n_sp, project, jnp.zeros((tok, width), F32))
        packed = jnp.concatenate([total[:half], total[half:]], axis=1)
        psum_send[...] = packed
        swap = pltpu.make_async_remote_copy(
            src_ref=psum_send, dst_ref=psum_recv, send_sem=ps_s, recv_sem=ps_r,
            device_id={"cfg": 1 - core}, device_id_type=MESH,
        )
        swap.start()
        swap.wait_recv()
        lat_mine[...] = (packed + psum_recv[...]).astype(BF16)

        def hand(step, carry):
            target = to_peer(step)
            pltpu.make_async_remote_copy(
                src_ref=lat_mine, dst_ref=lat_recv.at[me], send_sem=lat_s.at[target],
                recv_sem=lat_r.at[me], device_id={"section": 1, "sp": target},
                device_id_type=MESH,
            ).start()
            return carry

        lax.fori_loop(0, n_sp, hand, 0)

        def handed(step, carry):
            target = to_peer(step)
            pltpu.make_async_remote_copy(
                src_ref=lat_mine, dst_ref=lat_recv.at[me], send_sem=lat_s.at[target],
                recv_sem=lat_r.at[me], device_id={"section": 1, "sp": target},
                device_id_type=MESH,
            ).wait_send()
            return carry

        lax.fori_loop(0, n_sp, handed, 0)
        swap.wait_send()

    @pl.when(sec == 1)
    def _():
        def arrived(step, carry):
            branch_arrival(from_peer(step)).wait_recv()
            return carry

        lax.fori_loop(1, n_sp, arrived, 0)

        def latent_in(step, carry):
            source = from_peer(step)
            pltpu.make_async_remote_copy(
                src_ref=lat_mine, dst_ref=lat_recv.at[source], send_sem=lat_s.at[source],
                recv_sem=lat_r.at[source], device_id={"section": 0, "sp": source},
                device_id_type=MESH,
            ).wait_recv()
            return carry

        lax.fori_loop(0, n_sp, latent_in, 0)
        table = lat_recv[...].reshape(n_sp * half, 2 * width)
        low = jnp.dot(onehot[0], table, preferred_element_type=F32)
        high = jnp.dot(onehot[1], table, preferred_element_type=F32)
        lanes = lax.broadcasted_iota(jnp.int32, (tok, 2 * width), 1)
        picked = jnp.where(lanes < width, low, high).astype(BF16)

        def lift(g, carry):
            lifted = jnp.dot(picked, w2[g], preferred_element_type=F32)
            out_ref[g] = (brl[g].astype(F32) + lifted).astype(BF16)
            return carry

        lax.fori_loop(0, n_sp, lift, 0)

    def drain(step, carry):
        target = to_peer(step)
        for c in (0, 1, 2):
            qkv_copy(c, target).wait_send()
        branch_copy(target).wait_send()
        sibling_copy(target).wait_send()
        return carry

    lax.fori_loop(1, n_sp, drain, 0)
    sibling_copy(me).wait_send()


def on_device(qkv, counts, timesteps, block_map, w_out, w_in):
    n_sp = lax.axis_size("sp")
    tok, _, heads, hd = qkv.shape[2:]
    width = w_out.shape[2]
    seq = tok * n_sp
    half = tok // 2
    dma = pltpu.SemaphoreType.DMA
    smem = pl.BlockSpec(memory_space=pltpu.SMEM)
    vmem = pl.BlockSpec(memory_space=pltpu.VMEM)
    hbm = pl.BlockSpec(memory_space=pl.ANY)

    def body(*refs):
        kernel(n_sp, tok, heads, hd, width, *refs)

    by_head = pl.pallas_call(
        body,
        name="guided_attention",
        out_shape=jax.ShapeDtypeStruct((heads // 2, tok, hd), BF16),
        in_specs=[hbm, smem, smem, vmem, hbm, hbm],
        out_specs=vmem,
        scratch_shapes=[
            pltpu.VMEM((3, tok, heads, hd), BF16),
            pltpu.VMEM((3, heads, tok, hd), BF16),
            pltpu.VMEM((n_sp, 2, tok, hd), BF16),
            pltpu.VMEM((2, seq, hd), BF16),
            pltpu.VMEM((2, seq, 2 * hd), BF16),
            pltpu.VMEM((2, hd, seq), BF16),
            pltpu.VMEM((2, tok, seq), F32),
            pltpu.VMEM((n_sp, tok, hd), BF16),
            pltpu.VMEM((n_sp, tok, hd), BF16),
            pltpu.VMEM((n_sp, tok, hd), BF16),
            pltpu.VMEM((n_sp, tok, hd), BF16),
            pltpu.VMEM((n_sp, tok, hd), BF16),
            pltpu.VMEM((half, 2 * width), BF16),
            pltpu.VMEM((n_sp, half, 2 * width), BF16),
            pltpu.VMEM((half, 2 * width), F32),
            pltpu.VMEM((half, 2 * width), F32),
            pltpu.VMEM((2, tok, n_sp * half), BF16),
            pltpu.VMEM((heads, width, hd), BF16),
            pltpu.VMEM((width, heads, hd), BF16),
            pltpu.VMEM((heads // 2, 2 * width, hd), BF16),
            pltpu.VMEM((8, hd), F32),
            dma((3,)), dma((2,)), dma((3,)),
            dma((3, n_sp)), dma((3, n_sp)),
            dma((n_sp,)), dma((n_sp,)),
            dma((n_sp,)), dma((n_sp,)),
            dma, dma,
            dma((n_sp,)), dma((n_sp,)),
        ],
        compiler_params=pltpu.CompilerParams(
            collective_id=0, has_side_effects=True, vmem_limit_bytes=56 << 20
        ),
    )(
        qkv[0, 0],
        counts,
        timesteps,
        block_map.reshape(1, tok),
        jnp.swapaxes(w_out, 1, 2),
        w_in,
    )
    return jnp.swapaxes(by_head, 0, 1)[None, :, None]


def solution(mesh):
    placed = (
        P("section", "cfg", ("req", "sp"), None, None, None),
        P("section", "req"),
        P("section", "req"),
        P(("req", "sp")),
        P(),
        P(),
    )
    return jax.shard_map(
        on_device,
        mesh=mesh,
        in_specs=placed,
        out_specs=P("section", ("req", "sp"), "cfg", None, None),
        check_vma=False,
    )
```

time: 285 us -> 134 us (0.47)
  Pallas kernels: 0 us -> 128 us
  waiting for transfers between devices: 126 us -> 0 us
  matrix products: 60.3 us -> 0 us
  blocking collectives: 43.1 us -> 0 us
  local copies, waits for them, and re-layouts: 31.9 us -> 2.18 us
  starting transfers between devices: 17.3 us -> 0 us
  other arithmetic: 4.13 us -> 0 us
    pallas_call x0 -> x1, Pallas kernels: none -> 128 us  [on_device(): pl.pallas_call(body, name='guided_attention', out_shape=jax.ShapeDtypeStr...]
    all_to_all x2 -> x0, waiting for transfers between devices: 120 us -> none  [the longest x1 89.6 us: on_device(): lax.all_to_all(grouped, 'sp', split_axis=2, concat_axis=0, tiled=True)]
    sub x5 -> x0, matrix products: 38.7 us -> none  [one_block(): expo = jnp.where(keys_ok[None, None, :], jnp.exp(scores - top), 0.0)]
    all_gather x1 -> x0, blocking collectives: 34.6 us -> none  [on_device(): collected = lax.all_gather(latent, 'sp', axis=0, tiled=True)]
    dot_general x7 -> x0, matrix products: 21.6 us -> none  [the longest x5 20.2 us: one_block(): jnp.einsum('hqk,khd->qhd', expo.astype(jnp.bfloat16), values, preferred_e...]
    another operation x2 -> x0, local copies, waits for them, and re-layouts: 17.2 us -> none  [the longest x1 11.6 us: on_device(): attended = mixed_all[:, None]]
    all_to_all x2 -> x0, starting transfers between devices: 16.1 us -> none  [the longest x1 9.25 us: on_device(): lax.all_to_all(grouped, 'sp', split_axis=2, concat_axis=0, tiled=True)]
    ppermute x1 -> x0, waiting for transfers between devices: 6.1 us -> none  [passed_along(): lax.ppermute(value, axis, [(source, source + steps) for source in range(i...]
  transfers between devices with their start and end apart: 3 -> 0, of which waited for: 3 -> 0; matrix products, arithmetic and copies ran while one was open for 1% -> 0% of each run, Pallas kernels for 0% -> 0%
where the time goes in v1:
time: 134 us; the launch traced here: 132 us
  Pallas kernels  128 us (96%)
  local copies, waits for them, and re-layouts  2.18 us (2%)
    pallas_call x1, Pallas kernels, on_device(): pl.pallas_call(body, name='guided_attention', out_shape=jax.ShapeDtypeStr...  128 us

profile of v1, /device:TPU:20, one launch (start us, length us, event | category | flops | bytes accessed | tf_op | source)
XLA Modules:
  0.0 131.7 jit_solution(10725126736875874494)
XLA Ops:
  1.3 128.2 %guided_attention.1 = bf16[16,160,128]{2,1,0:T(8,128)(2,1)} custom-call(bf16[160,3,32,128]{3,2,1,0:T(8,128)(2,1)} %bitcast.6, s32[1,1]{1,0:T(1,128)S(6)} %copy.8.refs_1_, s32[1,1]{1,0:T(1,128)S(6)} %copy.9.refs_2_, s32[1,160]{1,0:T(1,128)} %bitcast.9, bf16[32,64,128]{2,1,0:T(8,128)(2,1)} %bitcast.8, bf16[64,32,128]{2,1,0:T(8,128)(2,1)} %refs_5_.1), custom_call_target="tpu_custom_call" | custom-call | tf_op jit(solution)/shard_map/guided_attention/pallas_call | solution.py:378
  129.5 2.2 %copy.7 = bf16[1,160,1,16,128]{4,3,2,1,0:T(8,128)(2,1)} copy(bf16[1,160,1,16,128]{4,1,3,2,0:T(8,128)(2,1)} %bitcast.7) | data formatting | bytes 1310720 | tf_op jit(solution)/shard_map/broadcast_in_dim | solution.py:424

commit v2 on v1

--- a/solution.py
+++ b/solution.py
@@ -10,22 +10,24 @@
 MESH = pl.DeviceIdType.MESH
 F32 = jnp.float32
 BF16 = jnp.bfloat16
+HOLD = 8
 
 
 def kernel(
     n_sp, tok, heads, hd, width,
     qkv_ref, cnt_ref, ts_ref, bm_ref, wo_ref, wi_ref, out_ref,
     xin, stage, qland, kland, vaug, kt, sc, att_mine, att_send, att_recv, brs, brl,
-    lat_mine, lat_recv, psum_send, psum_recv, onehot, wo, wi, w2, gate,
+    lat_mine, lat_a, lat_b, psum_send, psum_recv, onehot_a, onehot_b, wo, wi, w2, gate, lifted,
+    cnt, ts, bm,
     in_sem, w_sem, own_sem, s_sem, r_sem, sib_s, sib_r, br_s, br_r, ps_s, ps_r, lat_s, lat_r,
 ):
     seq = tok * n_sp
-    half = tok // 2
+    part_a = tok // 32 // 2 * 32 + tok // 32 % 2 * 32
+    parts = ((0, part_a), (part_a, tok - part_a))
     n_z = n_sp // 2
     sec = lax.axis_index("section")
     core = lax.axis_index("cfg")
     me = lax.axis_index("sp")
-    count = cnt_ref[0, 0]
     scale = hd ** -0.5 * math.log2(math.e)
 
     def offset(step):
@@ -44,21 +46,19 @@
     loads = [
         pltpu.make_async_copy(qkv_ref.at[:, c], xin.at[c], in_sem.at[c]) for c in (0, 1, 2)
     ]
-    for c in (1, 2, 0):
-        loads[c].start()
-    load_wo = pltpu.make_async_copy(wo_ref, wo, w_sem.at[0])
-    load_wi = pltpu.make_async_copy(wi_ref, wi, w_sem.at[1])
-    load_wo.start()
-    load_wi.start()
+    loads[1].start()
+    smalls = [
+        pltpu.make_async_copy(source, held, w_sem.at[n])
+        for n, (source, held) in enumerate(
+            ((wo_ref, wo), (wi_ref, wi), (cnt_ref, cnt), (ts_ref, ts), (bm_ref, bm))
+        )
+    ]
 
     barrier = pltpu.get_barrier_semaphore()
 
     def greet(step, carry):
         peer = to_peer(step)
         pl.semaphore_signal(barrier, inc=1, device_id={"sp": peer}, device_id_type=MESH)
-        pl.semaphore_signal(
-            barrier, inc=1, device_id={"section": 1 - sec, "sp": peer}, device_id_type=MESH
-        )
         return carry
 
     lax.fori_loop(1, n_sp, greet, 0)
@@ -115,8 +115,12 @@
         own_copy(c).start()
 
     loads[1].wait()
+    loads[2].start()
+    loads[0].start()
+    for small in smalls:
+        small.start()
     transpose_kind(1)
-    pl.semaphore_wait(barrier, 2 * n_sp)
+    pl.semaphore_wait(barrier, n_sp + 1)
     send_kind(1)
     loads[2].wait()
     transpose_kind(2)
@@ -125,18 +129,18 @@
     transpose_kind(0)
     send_kind(0)
 
+    for small in smalls:
+        small.wait()
+    count = cnt[0, 0]
     head_id = (2 * me + core).astype(F32)
     dims = lax.broadcasted_iota(jnp.int32, (8, hd), 1).astype(F32)
     freq = jnp.exp(-math.log(10000.0) * dims / hd)
-    gate[...] = 1.0 + 0.5 * jnp.sin(ts_ref[0, 0].astype(F32) * freq + 0.7 * head_id)
+    gate[...] = 1.0 + 0.5 * jnp.sin(ts[0, 0].astype(F32) * freq + 0.7 * head_id)
 
     key_rows = lax.broadcasted_iota(jnp.int32, (seq, hd), 0)
     ones = jnp.where(key_rows < count, 1.0, 0.0).astype(BF16)
     vaug[0, :, hd:] = ones
     vaug[1, :, hd:] = ones
-
-    load_wo.wait()
-    load_wi.wait()
 
     @pl.when(sec == 1)
     def _():
@@ -153,16 +157,21 @@
             jnp.int32, (tok, tok), 1
         )
         wanted = jnp.sum(
-            jnp.where(eye, jnp.broadcast_to(bm_ref[...], (tok, tok)).astype(F32), 0.0),
+            jnp.where(eye, jnp.broadcast_to(bm[...], (tok, tok)).astype(F32), 0.0),
             axis=1, keepdims=True,
         ).astype(jnp.int32)
         owner = wanted // tok
         row = wanted - owner * tok
-        upper = (row >= half).astype(jnp.int32)
-        slot = owner * half + row - upper * half
-        places = lax.broadcasted_iota(jnp.int32, (tok, n_sp * half), 1)
-        onehot[0] = jnp.where(places == jnp.where(upper == 0, slot, -1), 1.0, 0.0).astype(BF16)
-        onehot[1] = jnp.where(places == jnp.where(upper == 1, slot, -1), 1.0, 0.0).astype(BF16)
+        for onehot, (start, size) in ((onehot_a, parts[0]), (onehot_b, parts[1])):
+            depth = size // 2
+            inside = row - start
+            upper = (inside >= depth).astype(jnp.int32)
+            slot = owner * depth + inside - upper * depth
+            here = jnp.logical_and(inside >= 0, inside < size)
+            places = lax.broadcasted_iota(jnp.int32, (tok, n_sp * depth), 1)
+            for side in (0, 1):
+                target = jnp.where(jnp.logical_and(here, upper == side), slot, -1)
+                onehot[side] = jnp.where(places == target, 1.0, 0.0).astype(BF16)
 
     def wait_kind(c):
         def body(step, carry):
@@ -197,22 +206,24 @@
             device_id_type=MESH,
         )
 
-    def branch_copy(target):
-        return pltpu.make_async_remote_copy(
-            src_ref=brs.at[target],
-            dst_ref=brl.at[me],
-            send_sem=br_s.at[target],
-            recv_sem=br_r.at[me],
+    def branch_copy(part, target):
+        rows = pl.ds(*parts[part])
+        return pltpu.make_async_remote_copy(
+            src_ref=brs.at[target, rows],
+            dst_ref=brl.at[me, rows],
+            send_sem=br_s.at[part, target],
+            recv_sem=br_r.at[part, me],
             device_id={"sp": target},
             device_id_type=MESH,
         )
 
-    def branch_arrival(source):
-        return pltpu.make_async_remote_copy(
-            src_ref=brs.at[source],
-            dst_ref=brl.at[source],
-            send_sem=br_s.at[source],
-            recv_sem=br_r.at[source],
+    def branch_arrival(part, source):
+        rows = pl.ds(*parts[part])
+        return pltpu.make_async_remote_copy(
+            src_ref=brs.at[source, rows],
+            dst_ref=brl.at[source, rows],
+            send_sem=br_s.at[part, source],
+            recv_sem=br_r.at[part, source],
             device_id={"sp": source},
             device_id_type=MESH,
         )
@@ -242,10 +253,12 @@
         position = source * tok + lax.broadcasted_iota(jnp.int32, (tok, hd), 0)
         return source, jnp.where(position < count, gate[0:1] * guided, 0.0).astype(BF16)
 
-    def send_branch(step):
+    def keep(step):
         target, block = combine(step)
         brs[target] = block
-        branch_copy(target).start()
+
+    def send_part(part, step):
+        branch_copy(part, from_peer(step)).start()
 
     own_copy(0).wait()
     attend(0)
@@ -261,99 +274,142 @@
 
         @pl.when(step > 1)
         def _():
-            send_branch(step - 1)
+            keep(step - 1)
 
         return carry
 
-    lax.fori_loop(1, n_sp, first, 0)
-    send_branch(n_sp - 1)
+    def release(step, carry):
+        send_part(0, step)
+        return carry
+
+    def later(step, carry):
+        qkv_arrival(0, from_peer(step)).wait_recv()
+        attend(step)
+        keep(step - 1)
+        send_part(0, step - 1)
+        return carry
+
+    hold = n_sp - 1 if n_sp < HOLD else HOLD
+    lax.fori_loop(1, hold, first, 0)
+    lax.fori_loop(1, hold - 1, release, 0)
+    lax.fori_loop(hold, n_sp, later, 0)
+    keep(n_sp - 1)
+    send_part(0, n_sp - 1)
+
+    def second(step, carry):
+        send_part(1, step)
+        return carry
+
+    lax.fori_loop(1, n_sp, second, 0)
+
+    def swap_copy(part):
+        rows = pl.ds(parts[part][0] // 2, parts[part][1] // 2)
+        return pltpu.make_async_remote_copy(
+            src_ref=psum_send.at[rows], dst_ref=psum_recv.at[rows],
+            send_sem=ps_s.at[part], recv_sem=ps_r.at[part],
+            device_id={"cfg": 1 - core}, device_id_type=MESH,
+        )
+
+    def latent_copy(part, target):
+        rows = pl.ds(parts[part][0] // 2, parts[part][1] // 2)
+        return pltpu.make_async_remote_copy(
+            src_ref=lat_mine.at[rows], dst_ref=(lat_a, lat_b)[part].at[me],
+            send_sem=lat_s.at[part, target], recv_sem=lat_r.at[part, me],
+            device_id={"section": 1, "sp": target}, device_id_type=MESH,
+        )
+
+    def latent_arrival(part, source):
+        rows = pl.ds(parts[part][0] // 2, parts[part][1] // 2)
+        return pltpu.make_async_remote_copy(
+            src_ref=lat_mine.at[rows], dst_ref=(lat_a, lat_b)[part].at[source],
+            send_sem=lat_s.at[part, source], recv_sem=lat_r.at[part, source],
+            device_id={"section": 0, "sp": source}, device_id_type=MESH,
+        )
+
+    def turn_out(blocks):
+        def body(t, carry):
+            rows = pl.ds(pl.multiple_of(t * 16, 16), 16)
+            out_ref[rows] = jnp.swapaxes(blocks[:, rows, :], 0, 1)
+            return carry
+
+        lax.fori_loop(0, tok // 16, body, 0)
 
     @pl.when(sec == 0)
     def _():
-        def project(step, total):
-            source = from_peer(step)
-
-            @pl.when(step > 0)
-            def _():
-                branch_arrival(source).wait_recv()
-
-            block = brl[source]
-            out_ref[source] = block
-            return total + lax.dot_general(
-                block, wo[2 * source + core], (((1,), (1,)), ((), ())),
-                preferred_element_type=F32,
-            )
-
-        total = lax.fori_loop(0, n_sp, project, jnp.zeros((tok, width), F32))
-        packed = jnp.concatenate([total[:half], total[half:]], axis=1)
-        psum_send[...] = packed
-        swap = pltpu.make_async_remote_copy(
-            src_ref=psum_send, dst_ref=psum_recv, send_sem=ps_s, recv_sem=ps_r,
-            device_id={"cfg": 1 - core}, device_id_type=MESH,
-        )
-        swap.start()
-        swap.wait_recv()
-        lat_mine[...] = (packed + psum_recv[...]).astype(BF16)
-
-        def hand(step, carry):
-            target = to_peer(step)
-            pltpu.make_async_remote_copy(
-                src_ref=lat_mine, dst_ref=lat_recv.at[me], send_sem=lat_s.at[target],
-                recv_sem=lat_r.at[me], device_id={"section": 1, "sp": target},
-                device_id_type=MESH,
-            ).start()
-            return carry
-
-        lax.fori_loop(0, n_sp, hand, 0)
-
-        def handed(step, carry):
-            target = to_peer(step)
-            pltpu.make_async_remote_copy(
-                src_ref=lat_mine, dst_ref=lat_recv.at[me], send_sem=lat_s.at[target],
-                recv_sem=lat_r.at[me], device_id={"section": 1, "sp": target},
-                device_id_type=MESH,
-            ).wait_send()
-            return carry
-
-        lax.fori_loop(0, n_sp, handed, 0)
-        swap.wait_send()
+        for part, (start, size) in enumerate(parts):
+            def project(step, total, part=part, start=start, size=size):
+                source = from_peer(step)
+
+                @pl.when(step > 0)
+                def _():
+                    branch_arrival(part, source).wait_recv()
+
+                return total + lax.dot_general(
+                    brl[source, start:start + size], wo[2 * source + core],
+                    (((1,), (1,)), ((), ())), preferred_element_type=F32,
+                )
+
+            total = lax.fori_loop(0, n_sp, project, jnp.zeros((size, width), F32))
+            packed = jnp.concatenate([total[:size // 2], total[size // 2:]], axis=1)
+            rows = slice(start // 2, (start + size) // 2)
+            psum_send[rows] = packed
+            swap_copy(part).start()
+            swap_copy(part).wait_recv()
+            lat_mine[rows] = (packed + psum_recv[rows]).astype(BF16)
+
+            def hand(step, carry, part=part):
+                latent_copy(part, to_peer(step)).start()
+                return carry
+
+            lax.fori_loop(0, n_sp, hand, 0)
+
+        turn_out(brl)
+
+        for part in (0, 1):
+            def handed(step, carry, part=part):
+                latent_copy(part, to_peer(step)).wait_send()
+                return carry
+
+            lax.fori_loop(0, n_sp, handed, 0)
+            swap_copy(part).wait_send()
 
     @pl.when(sec == 1)
     def _():
+        lanes = lax.broadcasted_iota(jnp.int32, (tok, 2 * width), 1)
+
         def arrived(step, carry):
-            branch_arrival(from_peer(step)).wait_recv()
+            branch_arrival(0, from_peer(step)).wait_recv()
+            branch_arrival(1, from_peer(step)).wait_recv()
             return carry
 
         lax.fori_loop(1, n_sp, arrived, 0)
-
-        def latent_in(step, carry):
-            source = from_peer(step)
-            pltpu.make_async_remote_copy(
-                src_ref=lat_mine, dst_ref=lat_recv.at[source], send_sem=lat_s.at[source],
-                recv_sem=lat_r.at[source], device_id={"section": 0, "sp": source},
-                device_id_type=MESH,
-            ).wait_recv()
-            return carry
-
-        lax.fori_loop(0, n_sp, latent_in, 0)
-        table = lat_recv[...].reshape(n_sp * half, 2 * width)
-        low = jnp.dot(onehot[0], table, preferred_element_type=F32)
-        high = jnp.dot(onehot[1], table, preferred_element_type=F32)
-        lanes = lax.broadcasted_iota(jnp.int32, (tok, 2 * width), 1)
-        picked = jnp.where(lanes < width, low, high).astype(BF16)
+        picked = jnp.zeros((tok, 2 * width), F32)
+        for part, onehot, table in ((0, onehot_a, lat_a), (1, onehot_b, lat_b)):
+            def latent_in(step, carry, part=part):
+                latent_arrival(part, from_peer(step)).wait_recv()
+                return carry
+
+            lax.fori_loop(0, n_sp, latent_in, 0)
+            rows = table[...].reshape(n_sp * parts[part][1] // 2, 2 * width)
+            low = jnp.dot(onehot[0], rows, preferred_element_type=F32)
+            high = jnp.dot(onehot[1], rows, preferred_element_type=F32)
+            picked = picked + jnp.where(lanes < width, low, high)
+        wanted = picked.astype(BF16)
 
         def lift(g, carry):
-            lifted = jnp.dot(picked, w2[g], preferred_element_type=F32)
-            out_ref[g] = (brl[g].astype(F32) + lifted).astype(BF16)
+            raised = jnp.dot(wanted, w2[g], preferred_element_type=F32)
+            lifted[g] = (brl[g].astype(F32) + raised).astype(BF16)
             return carry
 
         lax.fori_loop(0, n_sp, lift, 0)
+        turn_out(lifted)
 
     def drain(step, carry):
         target = to_peer(step)
         for c in (0, 1, 2):
             qkv_copy(c, target).wait_send()
-        branch_copy(target).wait_send()
+        for part in (0, 1):
+            branch_copy(part, target).wait_send()
         sibling_copy(target).wait_send()
         return carry
 
@@ -367,19 +423,19 @@
     width = w_out.shape[2]
     seq = tok * n_sp
     half = tok // 2
+    half_a = (tok // 32 // 2 * 32 + tok // 32 % 2 * 32) // 2
     dma = pltpu.SemaphoreType.DMA
-    smem = pl.BlockSpec(memory_space=pltpu.SMEM)
     vmem = pl.BlockSpec(memory_space=pltpu.VMEM)
-    hbm = pl.BlockSpec(memory_space=pl.ANY)
+    hbm = pl.BlockSpec(memory_space=pltpu.HBM)
 
     def body(*refs):
         kernel(n_sp, tok, heads, hd, width, *refs)
 
-    by_head = pl.pallas_call(
+    result = pl.pallas_call(
         body,
         name="guided_attention",
-        out_shape=jax.ShapeDtypeStruct((heads // 2, tok, hd), BF16),
-        in_specs=[hbm, smem, smem, vmem, hbm, hbm],
+        out_shape=jax.ShapeDtypeStruct((tok, heads // 2, hd), BF16),
+        in_specs=[hbm] * 6,
         out_specs=vmem,
         scratch_shapes=[
             pltpu.VMEM((3, tok, heads, hd), BF16),
@@ -395,20 +451,26 @@
             pltpu.VMEM((n_sp, tok, hd), BF16),
             pltpu.VMEM((n_sp, tok, hd), BF16),
             pltpu.VMEM((half, 2 * width), BF16),
-            pltpu.VMEM((n_sp, half, 2 * width), BF16),
+            pltpu.VMEM((n_sp, half_a, 2 * width), BF16),
+            pltpu.VMEM((n_sp, half - half_a, 2 * width), BF16),
             pltpu.VMEM((half, 2 * width), F32),
             pltpu.VMEM((half, 2 * width), F32),
-            pltpu.VMEM((2, tok, n_sp * half), BF16),
+            pltpu.VMEM((2, tok, n_sp * half_a), BF16),
+            pltpu.VMEM((2, tok, n_sp * (half - half_a)), BF16),
             pltpu.VMEM((heads, width, hd), BF16),
             pltpu.VMEM((width, heads, hd), BF16),
             pltpu.VMEM((heads // 2, 2 * width, hd), BF16),
             pltpu.VMEM((8, hd), F32),
-            dma((3,)), dma((2,)), dma((3,)),
+            pltpu.VMEM((heads // 2, tok, hd), BF16),
+            pltpu.SMEM((1, 1), jnp.int32),
+            pltpu.SMEM((1, 1), jnp.int32),
+            pltpu.VMEM((1, tok), jnp.int32),
+            dma((3,)), dma((5,)), dma((3,)),
             dma((3, n_sp)), dma((3, n_sp)),
             dma((n_sp,)), dma((n_sp,)),
-            dma((n_sp,)), dma((n_sp,)),
-            dma, dma,
-            dma((n_sp,)), dma((n_sp,)),
+            dma((2, n_sp)), dma((2, n_sp)),
+            dma((2,)), dma((2,)),
+            dma((2, n_sp)), dma((2, n_sp)),
         ],
         compiler_params=pltpu.CompilerParams(
             collective_id=0, has_side_effects=True, vmem_limit_bytes=56 << 20
@@ -421,7 +483,7 @@
         jnp.swapaxes(w_out, 1, 2),
         w_in,
     )
-    return jnp.swapaxes(by_head, 0, 1)[None, :, None]
+    return result[None, :, None]
 
 
 def solution(mesh):

time: 134 us -> 132 us (0.985); the launches traced: 132 us -> 131 us
    broadcast_in_dim x1 -> x0, local copies, waits for them, and re-layouts: 2.18 us -> none  [on_device(): return jnp.swapaxes(by_head, 0, 1)[None, :, None]]
    unnamed x0 -> x1, local copies, waits for them, and re-layouts: none -> 2.04 us
where the time goes in v2:
time: 132 us; the launch traced here: 131 us
  Pallas kernels  128 us (97%)
  local copies, waits for them, and re-layouts  2.04 us (2%)
    pallas_call x1, Pallas kernels, on_device(): pl.pallas_call(body, name='guided_attention', out_shape=jax.ShapeDtypeStr...  128 us

profile of v2, /device:TPU:20, one launch (start us, length us, event | category | flops | bytes accessed | tf_op | source)
XLA Modules:
  0.0 131.5 jit_solution(6341308982628589477)
XLA Ops:
  1.3 128.1 %guided_attention.1 = bf16[160,16,128]{2,1,0:T(8,128)(2,1)} custom-call(bf16[160,3,32,128]{3,2,1,0:T(8,128)(2,1)} %bitcast.6, s32[1,1]{1,0:T(1,128)S(6)} %copy.9.refs_1_, s32[1,1]{1,0:T(1,128)S(6)} %copy.10.refs_2_, s32[1,160]{1,0:T(1,128)} %bitcast.9, bf16[32,64,128]{2,1,0:T(8,128)(2,1)} %bitcast.8, bf16[64,32,128]{2,1,0:T(8,128)(2,1)} %refs_5_.1), custom_call_target="tpu_custom_call" | custom-call | tf_op jit(solution)/shard_map/guided_attention/pallas_call | solution.py:434
  129.4 2.0 %copy.11 = bf16[1,160,1,16,128]{4,3,2,1,0:T(8,128)(2,1)} copy(bf16[1,160,1,16,128]{4,3,2,1,0:T(8,128)(2,1)} %bitcast.7) | data formatting | bytes 1310720

commit v3 on v2

--- a/solution.py
+++ b/solution.py
@@ -10,20 +10,30 @@
 MESH = pl.DeviceIdType.MESH
 F32 = jnp.float32
 BF16 = jnp.bfloat16
-HOLD = 8
+HOLD = 12
+RELAYED = (1,)
+
+
+def part_rows(tok):
+    steps = tok // 32
+    sizes = (32 * (steps * 3 // 5), 32 * (steps - 1 - steps * 3 // 5), 32)
+    return tuple((sum(sizes[:n]), size) for n, size in enumerate(sizes))
 
 
 def kernel(
     n_sp, tok, heads, hd, width,
-    qkv_ref, cnt_ref, ts_ref, bm_ref, wo_ref, wi_ref, out_ref,
-    xin, stage, qland, kland, vaug, kt, sc, att_mine, att_send, att_recv, brs, brl,
-    lat_mine, lat_a, lat_b, psum_send, psum_recv, onehot_a, onehot_b, wo, wi, w2, gate, lifted,
+    qkv_ref, cnt_ref, ts_ref, bm_ref, wo_ref, wi_ref, brl_out, wanted_out, w2_out,
+    xin, stage, qland, kland, vaug, kt, sc, att_mine, att_send, att_recv, brs, brl, relay,
+    lat_mine, lat_a, lat_b, lat_c, psum_send, psum_recv, onehot_a, onehot_b, onehot_c, wo, wi, gate,
+    wanted_held, w2,
     cnt, ts, bm,
     in_sem, w_sem, own_sem, s_sem, r_sem, sib_s, sib_r, br_s, br_r, ps_s, ps_r, lat_s, lat_r,
+    relay_s, relay_r, out_sem,
 ):
     seq = tok * n_sp
-    part_a = tok // 32 // 2 * 32 + tok // 32 % 2 * 32
-    parts = ((0, part_a), (part_a, tok - part_a))
+    parts = part_rows(tok)
+    tables = (lat_a, lat_b, lat_c)
+    onehots = (onehot_a, onehot_b, onehot_c)
     n_z = n_sp // 2
     sec = lax.axis_index("section")
     core = lax.axis_index("cfg")
@@ -39,9 +49,16 @@
         dx, dz = offset(step)
         return ((me // n_z + dx) % 2) * n_z + (me % n_z + dz + n_z) % n_z
 
+    def query_peer(step):
+        return from_peer(step)
+
     def from_peer(step):
         dx, dz = offset(step)
         return ((me // n_z + dx) % 2) * n_z + (me % n_z - dz + n_z) % n_z
+
+    across = n_sp - 2
+    mirror = (1 - me // n_z) * n_z + me % n_z
+    mirror_opposite = (1 - me // n_z) * n_z + (me % n_z + n_z // 2) % n_z
 
     loads = [
         pltpu.make_async_copy(qkv_ref.at[:, c], xin.at[c], in_sem.at[c]) for c in (0, 1, 2)
@@ -63,7 +80,10 @@
 
     lax.fori_loop(1, n_sp, greet, 0)
     pl.semaphore_signal(barrier, inc=1, device_id={"cfg": 1 - core}, device_id_type=MESH)
-    pl.semaphore_signal(barrier, inc=1, device_id={"section": 1 - sec}, device_id_type=MESH)
+    for peer in (mirror, mirror_opposite):
+        pl.semaphore_signal(
+            barrier, inc=1, device_id={"section": 1 - sec, "sp": peer}, device_id_type=MESH
+        )
 
     def transpose_kind(c):
         def body(t, carry):
@@ -120,14 +140,75 @@
     for small in smalls:
         small.start()
     transpose_kind(1)
-    pl.semaphore_wait(barrier, n_sp + 1)
-    send_kind(1)
     loads[2].wait()
     transpose_kind(2)
-    send_kind(2)
+    pl.semaphore_wait(barrier, n_sp + 2)
+
+    def to_relay(c):
+        target = to_peer(across)
+        return pltpu.make_async_remote_copy(
+            src_ref=stage.at[c, pl.ds(2 * target, 2)],
+            dst_ref=relay.at[c - 1],
+            send_sem=s_sem.at[c, target],
+            recv_sem=relay_r.at[c - 1],
+            device_id={"section": 1, "sp": mirror},
+            device_id_type=MESH,
+        )
+
+    def onward(c):
+        return pltpu.make_async_remote_copy(
+            src_ref=relay.at[c - 1],
+            dst_ref=landing(c, mirror),
+            send_sem=relay_s.at[c - 1],
+            recv_sem=r_sem.at[c, mirror],
+            device_id={"section": 0, "sp": mirror_opposite},
+            device_id_type=MESH,
+        )
+
+    def relay_in(c):
+        return pltpu.make_async_remote_copy(
+            src_ref=relay.at[c - 1],
+            dst_ref=relay.at[c - 1],
+            send_sem=relay_s.at[c - 1],
+            recv_sem=relay_r.at[c - 1],
+            device_id={"section": 0, "sp": mirror},
+            device_id_type=MESH,
+        )
+
+    def send_most(c):
+        def body(step, carry):
+            @pl.when(jnp.logical_or(sec == 1, step != across))
+            def _():
+                qkv_copy(c, to_peer(step)).start()
+
+            return carry
+
+        lax.fori_loop(1, n_sp, body, 0)
+        own_copy(c).start()
+
+    @pl.when(sec == 0)
+    def _():
+        for c in RELAYED:
+            to_relay(c).start()
+
+    (send_most if 1 in RELAYED else send_kind)(1)
+
+    @pl.when(sec == 1)
+    def _():
+        for c in RELAYED:
+            relay_in(c).wait_recv()
+            onward(c).start()
+
+    (send_most if 2 in RELAYED else send_kind)(2)
     loads[0].wait()
     transpose_kind(0)
-    send_kind(0)
+
+    def send_query(step, carry):
+        qkv_copy(0, to_peer(step)).start()
+        return carry
+
+    lax.fori_loop(1, n_sp, send_query, 0)
+    own_copy(0).start()
 
     for small in smalls:
         small.wait()
@@ -142,17 +223,18 @@
     vaug[0, :, hd:] = ones
     vaug[1, :, hd:] = ones
 
+    for t in range(width // 16):
+        stacked = jnp.swapaxes(wi[t * 16:t * 16 + 16], 0, 1).reshape(heads // 2, 2, 16, hd)
+        chosen = jnp.where(core == 0, stacked[:, 0], stacked[:, 1])
+        for g in range(heads // 2):
+            for copy in (0, width):
+                w2[copy + t * 16:copy + t * 16 + 16, g * hd:(g + 1) * hd] = chosen[g]
+
+    w2_copy = pltpu.make_async_copy(w2, w2_out, out_sem.at[0])
+    w2_copy.start()
+
     @pl.when(sec == 1)
     def _():
-        def turn(t, carry):
-            rows = pl.ds(pl.multiple_of(t * 16, 16), 16)
-            stacked = jnp.swapaxes(wi[rows], 0, 1).reshape(heads // 2, 2, 16, hd)
-            part = jnp.where(core == 0, stacked[:, 0], stacked[:, 1])
-            w2[:, rows, :] = part
-            w2[:, pl.ds(pl.multiple_of(width + t * 16, 16), 16), :] = part
-            return carry
-
-        lax.fori_loop(0, width // 16, turn, 0)
         eye = lax.broadcasted_iota(jnp.int32, (tok, tok), 0) == lax.broadcasted_iota(
             jnp.int32, (tok, tok), 1
         )
@@ -162,7 +244,7 @@
         ).astype(jnp.int32)
         owner = wanted // tok
         row = wanted - owner * tok
-        for onehot, (start, size) in ((onehot_a, parts[0]), (onehot_b, parts[1])):
+        for onehot, (start, size) in zip(onehots, parts):
             depth = size // 2
             inside = row - start
             upper = (inside >= depth).astype(jnp.int32)
@@ -229,7 +311,7 @@
         )
 
     def attend(step):
-        source = from_peer(step)
+        source = query_peer(step)
         for h in (0, 1):
             sc[h] = jnp.dot(qland[source, h], kt[h], preferred_element_type=F32)
         done = []
@@ -243,7 +325,7 @@
         sibling_copy(source).start()
 
     def combine(step):
-        source = from_peer(step)
+        source = query_peer(step)
         sibling_copy(source).wait_recv()
         mine = att_mine[source].astype(F32)
         theirs = att_recv[source].astype(F32)
@@ -258,13 +340,13 @@
         brs[target] = block
 
     def send_part(part, step):
-        branch_copy(part, from_peer(step)).start()
+        branch_copy(part, query_peer(step)).start()
 
     own_copy(0).wait()
     attend(0)
 
     def first(step, carry):
-        qkv_arrival(0, from_peer(step)).wait_recv()
+        qkv_arrival(0, query_peer(step)).wait_recv()
         attend(step)
 
         @pl.when(step == 1)
@@ -283,7 +365,7 @@
         return carry
 
     def later(step, carry):
-        qkv_arrival(0, from_peer(step)).wait_recv()
+        qkv_arrival(0, query_peer(step)).wait_recv()
         attend(step)
         keep(step - 1)
         send_part(0, step - 1)
@@ -296,11 +378,12 @@
     keep(n_sp - 1)
     send_part(0, n_sp - 1)
 
-    def second(step, carry):
-        send_part(1, step)
-        return carry
-
-    lax.fori_loop(1, n_sp, second, 0)
+    for part in range(1, len(parts)):
+        def send_rest(step, carry, part=part):
+            send_part(part, step)
+            return carry
+
+        lax.fori_loop(1, n_sp, send_rest, 0)
 
     def swap_copy(part):
         rows = pl.ds(parts[part][0] // 2, parts[part][1] // 2)
@@ -313,7 +396,7 @@
     def latent_copy(part, target):
         rows = pl.ds(parts[part][0] // 2, parts[part][1] // 2)
         return pltpu.make_async_remote_copy(
-            src_ref=lat_mine.at[rows], dst_ref=(lat_a, lat_b)[part].at[me],
+            src_ref=lat_mine.at[rows], dst_ref=tables[part].at[me],
             send_sem=lat_s.at[part, target], recv_sem=lat_r.at[part, me],
             device_id={"section": 1, "sp": target}, device_id_type=MESH,
         )
@@ -321,35 +404,43 @@
     def latent_arrival(part, source):
         rows = pl.ds(parts[part][0] // 2, parts[part][1] // 2)
         return pltpu.make_async_remote_copy(
-            src_ref=lat_mine.at[rows], dst_ref=(lat_a, lat_b)[part].at[source],
+            src_ref=lat_mine.at[rows], dst_ref=tables[part].at[source],
             send_sem=lat_s.at[part, source], recv_sem=lat_r.at[part, source],
             device_id={"section": 0, "sp": source}, device_id_type=MESH,
         )
 
-    def turn_out(blocks):
-        def body(t, carry):
-            rows = pl.ds(pl.multiple_of(t * 16, 16), 16)
-            out_ref[rows] = jnp.swapaxes(blocks[:, rows, :], 0, 1)
-            return carry
-
-        lax.fori_loop(0, tok // 16, body, 0)
+    def drain(step, carry):
+        target = to_peer(step)
+        for c in (0, 1, 2):
+            qkv_copy(c, target).wait_send()
+        sibling_copy(target).wait_send()
+        return carry
+
+    lax.fori_loop(1, n_sp, drain, 0)
+    sibling_copy(me).wait_send()
+
+    def drain_branch(step, carry):
+        for part in range(len(parts)):
+            branch_copy(part, to_peer(step)).wait_send()
+        return carry
+
+    wanted_copy = pltpu.make_async_copy(wanted_held, wanted_out, out_sem.at[1])
+    brl_copy = pltpu.make_async_copy(brl, brl_out, out_sem.at[2])
 
     @pl.when(sec == 0)
     def _():
         for part, (start, size) in enumerate(parts):
-            def project(step, total, part=part, start=start, size=size):
-                source = from_peer(step)
-
-                @pl.when(step > 0)
-                def _():
-                    branch_arrival(part, source).wait_recv()
-
-                return total + lax.dot_general(
+            def returned(step, carry, part=part):
+                branch_arrival(part, from_peer(step)).wait_recv()
+                return carry
+
+            lax.fori_loop(1, n_sp, returned, 0)
+            total = jnp.zeros((size, width), F32)
+            for source in range(n_sp):
+                total = total + lax.dot_general(
                     brl[source, start:start + size], wo[2 * source + core],
                     (((1,), (1,)), ((), ())), preferred_element_type=F32,
                 )
-
-            total = lax.fori_loop(0, n_sp, project, jnp.zeros((size, width), F32))
             packed = jnp.concatenate([total[:size // 2], total[size // 2:]], axis=1)
             rows = slice(start // 2, (start + size) // 2)
             psum_send[rows] = packed
@@ -363,9 +454,11 @@
 
             lax.fori_loop(0, n_sp, hand, 0)
 
-        turn_out(brl)
-
-        for part in (0, 1):
+        wanted_held[...] = jnp.zeros_like(wanted_held)
+        wanted_copy.start()
+        brl_copy.start()
+        lax.fori_loop(1, n_sp, drain_branch, 0)
+        for part in range(len(parts)):
             def handed(step, carry, part=part):
                 latent_copy(part, to_peer(step)).wait_send()
                 return carry
@@ -378,13 +471,15 @@
         lanes = lax.broadcasted_iota(jnp.int32, (tok, 2 * width), 1)
 
         def arrived(step, carry):
-            branch_arrival(0, from_peer(step)).wait_recv()
-            branch_arrival(1, from_peer(step)).wait_recv()
+            for part in range(len(parts)):
+                branch_arrival(part, from_peer(step)).wait_recv()
             return carry
 
         lax.fori_loop(1, n_sp, arrived, 0)
+        brl_copy.start()
+        lax.fori_loop(1, n_sp, drain_branch, 0)
         picked = jnp.zeros((tok, 2 * width), F32)
-        for part, onehot, table in ((0, onehot_a, lat_a), (1, onehot_b, lat_b)):
+        for part, (onehot, table) in enumerate(zip(onehots, tables)):
             def latent_in(step, carry, part=part):
                 latent_arrival(part, from_peer(step)).wait_recv()
                 return carry
@@ -394,27 +489,29 @@
             low = jnp.dot(onehot[0], rows, preferred_element_type=F32)
             high = jnp.dot(onehot[1], rows, preferred_element_type=F32)
             picked = picked + jnp.where(lanes < width, low, high)
-        wanted = picked.astype(BF16)
-
-        def lift(g, carry):
-            raised = jnp.dot(wanted, w2[g], preferred_element_type=F32)
-            lifted[g] = (brl[g].astype(F32) + raised).astype(BF16)
-            return carry
-
-        lax.fori_loop(0, n_sp, lift, 0)
-        turn_out(lifted)
-
-    def drain(step, carry):
-        target = to_peer(step)
-        for c in (0, 1, 2):
-            qkv_copy(c, target).wait_send()
-        for part in (0, 1):
-            branch_copy(part, target).wait_send()
-        sibling_copy(target).wait_send()
-        return carry
-
-    lax.fori_loop(1, n_sp, drain, 0)
-    sibling_copy(me).wait_send()
+        wanted_held[...] = picked.astype(BF16)
+        wanted_copy.start()
+
+    w2_copy.wait()
+    brl_copy.wait()
+    wanted_copy.wait()
+
+    @pl.when(sec == 1)
+    def _():
+        for c in RELAYED:
+            onward(c).wait_send()
+
+
+def lift_kernel(wanted_ref, w2_ref, brl_ref, out_ref):
+    groups, _, hd = brl_ref.shape
+    raised = jnp.dot(wanted_ref[...], w2_ref[...], preferred_element_type=F32)
+    result = jnp.stack(
+        [
+            (brl_ref[g].astype(F32) + raised[:, g * hd:(g + 1) * hd]).astype(BF16)
+            for g in range(groups)
+        ]
+    )
+    out_ref[...] = jnp.swapaxes(result, 0, 1)
 
 
 def on_device(qkv, counts, timesteps, block_map, w_out, w_in):
@@ -423,20 +520,23 @@
     width = w_out.shape[2]
     seq = tok * n_sp
     half = tok // 2
-    half_a = (tok // 32 // 2 * 32 + tok // 32 % 2 * 32) // 2
+    halves = [size // 2 for _, size in part_rows(tok)]
     dma = pltpu.SemaphoreType.DMA
-    vmem = pl.BlockSpec(memory_space=pltpu.VMEM)
     hbm = pl.BlockSpec(memory_space=pltpu.HBM)
 
     def body(*refs):
         kernel(n_sp, tok, heads, hd, width, *refs)
 
-    result = pl.pallas_call(
+    brl, wanted, w2 = pl.pallas_call(
         body,
         name="guided_attention",
-        out_shape=jax.ShapeDtypeStruct((tok, heads // 2, hd), BF16),
+        out_shape=(
+            jax.ShapeDtypeStruct((n_sp, tok, hd), BF16),
+            jax.ShapeDtypeStruct((tok, 2 * width), BF16),
+            jax.ShapeDtypeStruct((2 * width, heads // 2 * hd), BF16),
+        ),
         in_specs=[hbm] * 6,
-        out_specs=vmem,
+        out_specs=(hbm, hbm, hbm),
         scratch_shapes=[
             pltpu.VMEM((3, tok, heads, hd), BF16),
             pltpu.VMEM((3, heads, tok, hd), BF16),
@@ -450,27 +550,27 @@
             pltpu.VMEM((n_sp, tok, hd), BF16),
             pltpu.VMEM((n_sp, tok, hd), BF16),
             pltpu.VMEM((n_sp, tok, hd), BF16),
+            pltpu.VMEM((2, 2, tok, hd), BF16),
             pltpu.VMEM((half, 2 * width), BF16),
-            pltpu.VMEM((n_sp, half_a, 2 * width), BF16),
-            pltpu.VMEM((n_sp, half - half_a, 2 * width), BF16),
+            *[pltpu.VMEM((n_sp, depth, 2 * width), BF16) for depth in halves],
             pltpu.VMEM((half, 2 * width), F32),
             pltpu.VMEM((half, 2 * width), F32),
-            pltpu.VMEM((2, tok, n_sp * half_a), BF16),
-            pltpu.VMEM((2, tok, n_sp * (half - half_a)), BF16),
+            *[pltpu.VMEM((2, tok, n_sp * depth), BF16) for depth in halves],
             pltpu.VMEM((heads, width, hd), BF16),
             pltpu.VMEM((width, heads, hd), BF16),
-            pltpu.VMEM((heads // 2, 2 * width, hd), BF16),
             pltpu.VMEM((8, hd), F32),
-            pltpu.VMEM((heads // 2, tok, hd), BF16),
+            pltpu.VMEM((tok, 2 * width), BF16),
+            pltpu.VMEM((2 * width, heads // 2 * hd), BF16),
             pltpu.SMEM((1, 1), jnp.int32),
             pltpu.SMEM((1, 1), jnp.int32),
             pltpu.VMEM((1, tok), jnp.int32),
             dma((3,)), dma((5,)), dma((3,)),
             dma((3, n_sp)), dma((3, n_sp)),
             dma((n_sp,)), dma((n_sp,)),
-            dma((2, n_sp)), dma((2, n_sp)),
-            dma((2,)), dma((2,)),
-            dma((2, n_sp)), dma((2, n_sp)),
+            dma((3, n_sp)), dma((3, n_sp)),
+            dma((3,)), dma((3,)),
+            dma((3, n_sp)), dma((3, n_sp)),
+            dma((2,)), dma((2,)), dma((3,)),
         ],
         compiler_params=pltpu.CompilerParams(
             collective_id=0, has_side_effects=True, vmem_limit_bytes=56 << 20
@@ -483,6 +583,11 @@
         jnp.swapaxes(w_out, 1, 2),
         w_in,
     )
+    result = pl.pallas_call(
+        lift_kernel,
+        name="lift",
+        out_shape=jax.ShapeDtypeStruct((tok, heads // 2, hd), BF16),
+    )(wanted, w2, brl)
     return result[None, :, None]
 
 

time: 132 us -> 125 us (0.947)
  Pallas kernels: 128 us -> 123 us
  local copies, waits for them, and re-layouts: 2.04 us -> 0 us
    pallas_call x1 -> x2, Pallas kernels: 128 us -> 123 us  [the longest x1 120 us: on_device(): pl.pallas_call(body, name='guided_attention', out_shape=(jax.ShapeDtypeSt...]
    unnamed x1 -> x0, local copies, waits for them, and re-layouts: 2.04 us -> none
where the time goes in v3:
time: 125 us; the launch traced here: 124 us
  Pallas kernels  123 us (98%)
  between operations  1.3 us (1%)
    pallas_call x1, Pallas kernels, on_device(): pl.pallas_call(body, name='guided_attention', out_shape=(jax.ShapeDtypeSt...  120 us

profile of v3, /device:TPU:20, one launch (start us, length us, event | category | flops | bytes accessed | tf_op | source)
XLA Modules:
  0.0 123.9 jit_solution(10637185557588270428)
XLA Ops:
  1.3 120.1 %guided_attention.1 = (bf16[16,160,128]{2,1,0:T(8,128)(2,1)}, bf16[160,128]{1,0:T(8,128)(2,1)}, bf16[128,2048]{1,0:T(8,128)(2,1)}) custom-call(bf16[160,3,32,128]{3,2,1,0:T(8,128)(2,1)} %bitcast.6, s32[1,1]{1,0:T(1,128)S(6)} %copy.8.refs_1_, s32[1,1]{1,0:T(1,128)S(6)} %copy.9.refs_2_, s32[1,160]{1,0:T(1,128)} %bitcast.8, bf16[32,64,128]{2,1,0:T(8,128)(2,1)} %bitcast.7, ...), custom_call_target="tpu_custom_call" | custom-call | tf_op jit(solution)/shard_map/guided_attention/pallas_call | solution.py:530
  121.4 2.4 %lift.1 = bf16[160,16,128]{2,1,0:T(8,128)(2,1)} custom-call(bf16[160,128]{1,0:T(8,128)(2,1)} %get-tuple-element.8.wanted_ref, bf16[128,2048]{1,0:T(8,128)(2,1)} %get-tuple-element.9.w2_ref, bf16[16,160,128]{2,1,0:T(8,128)(2,1)} %get-tuple-element.10.brl_ref), custom_call_target="tpu_custom_call" | custom-call | tf_op jit(solution)/shard_map/lift/pallas_call | solution.py:586

commit v4 on v3

--- a/solution.py
+++ b/solution.py
@@ -27,7 +27,7 @@
     lat_mine, lat_a, lat_b, lat_c, psum_send, psum_recv, onehot_a, onehot_b, onehot_c, wo, wi, gate,
     wanted_held, w2,
     cnt, ts, bm,
-    in_sem, w_sem, own_sem, s_sem, r_sem, sib_s, sib_r, br_s, br_r, ps_s, ps_r, lat_s, lat_r,
+    in_sem, w_sem, own_sem, s_sem, r_sem, q_sem, sib_s, sib_r, br_s, br_r, ps_s, ps_r, lat_s, lat_r,
     relay_s, relay_r, out_sem,
 ):
     seq = tok * n_sp
@@ -105,21 +105,33 @@
         return pltpu.make_async_remote_copy(
             src_ref=stage.at[c, pl.ds(2 * target, 2)],
             dst_ref=landing(c, me),
-            send_sem=s_sem.at[c, target],
-            recv_sem=r_sem.at[c, me],
+            send_sem=s_sem.at[c],
+            recv_sem=q_sem.at[me] if c == 0 else r_sem.at[c],
             device_id={"sp": target},
             device_id_type=MESH,
         )
 
-    def qkv_arrival(c, source):
-        return pltpu.make_async_remote_copy(
-            src_ref=stage.at[c, pl.ds(2 * source, 2)],
-            dst_ref=landing(c, source),
-            send_sem=s_sem.at[c, source],
-            recv_sem=r_sem.at[c, source],
+    def query_arrival(source):
+        return pltpu.make_async_remote_copy(
+            src_ref=qland.at[source],
+            dst_ref=qland.at[source],
+            send_sem=s_sem.at[0],
+            recv_sem=q_sem.at[source],
             device_id={"sp": source},
             device_id_type=MESH,
         )
+
+    def all_sent(held, sem):
+        pltpu.make_async_remote_copy(
+            src_ref=held, dst_ref=held, send_sem=sem, recv_sem=sem,
+            device_id={"cfg": 1 - core}, device_id_type=MESH,
+        ).wait_send()
+
+    def all_arrived(held, sem):
+        pltpu.make_async_remote_copy(
+            src_ref=held, dst_ref=held, send_sem=sem, recv_sem=sem,
+            device_id={"cfg": 1 - core}, device_id_type=MESH,
+        ).wait_recv()
 
     def own_copy(c):
         return pltpu.make_async_copy(
@@ -149,7 +161,7 @@
         return pltpu.make_async_remote_copy(
             src_ref=stage.at[c, pl.ds(2 * target, 2)],
             dst_ref=relay.at[c - 1],
-            send_sem=s_sem.at[c, target],
+            send_sem=s_sem.at[c],
             recv_sem=relay_r.at[c - 1],
             device_id={"section": 1, "sp": mirror},
             device_id_type=MESH,
@@ -160,7 +172,7 @@
             src_ref=relay.at[c - 1],
             dst_ref=landing(c, mirror),
             send_sem=relay_s.at[c - 1],
-            recv_sem=r_sem.at[c, mirror],
+            recv_sem=r_sem.at[c],
             device_id={"section": 0, "sp": mirror_opposite},
             device_id_type=MESH,
         )
@@ -255,12 +267,12 @@
                 target = jnp.where(jnp.logical_and(here, upper == side), slot, -1)
                 onehot[side] = jnp.where(places == target, 1.0, 0.0).astype(BF16)
 
+    others = pl.ds(0, (n_sp - 1) * tok)
+
     def wait_kind(c):
-        def body(step, carry):
-            qkv_arrival(c, from_peer(step)).wait_recv()
-            return carry
-
-        lax.fori_loop(1, n_sp, body, 0)
+        all_arrived(
+            kland.at[:, others] if c == 1 else vaug.at[:, others, pl.ds(0, hd)], r_sem.at[c]
+        )
         own_copy(c).wait()
 
     quarter = seq // 4
@@ -282,7 +294,7 @@
         return pltpu.make_async_remote_copy(
             src_ref=att_send.at[source],
             dst_ref=att_recv.at[source],
-            send_sem=sib_s.at[source],
+            send_sem=sib_s,
             recv_sem=sib_r.at[source],
             device_id={"cfg": 1 - core},
             device_id_type=MESH,
@@ -293,22 +305,14 @@
         return pltpu.make_async_remote_copy(
             src_ref=brs.at[target, rows],
             dst_ref=brl.at[me, rows],
-            send_sem=br_s.at[part, target],
-            recv_sem=br_r.at[part, me],
+            send_sem=br_s.at[part],
+            recv_sem=br_r.at[part],
             device_id={"sp": target},
             device_id_type=MESH,
         )
 
-    def branch_arrival(part, source):
-        rows = pl.ds(*parts[part])
-        return pltpu.make_async_remote_copy(
-            src_ref=brs.at[source, rows],
-            dst_ref=brl.at[source, rows],
-            send_sem=br_s.at[part, source],
-            recv_sem=br_r.at[part, source],
-            device_id={"sp": source},
-            device_id_type=MESH,
-        )
+    def branches(blocks, part):
+        return blocks.at[pl.ds(0, n_sp - 1), pl.ds(*parts[part])]
 
     def attend(step):
         source = query_peer(step)
@@ -346,7 +350,7 @@
     attend(0)
 
     def first(step, carry):
-        qkv_arrival(0, query_peer(step)).wait_recv()
+        query_arrival(query_peer(step)).wait_recv()
         attend(step)
 
         @pl.when(step == 1)
@@ -365,7 +369,7 @@
         return carry
 
     def later(step, carry):
-        qkv_arrival(0, query_peer(step)).wait_recv()
+        query_arrival(query_peer(step)).wait_recv()
         attend(step)
         keep(step - 1)
         send_part(0, step - 1)
@@ -397,32 +401,13 @@
         rows = pl.ds(parts[part][0] // 2, parts[part][1] // 2)
         return pltpu.make_async_remote_copy(
             src_ref=lat_mine.at[rows], dst_ref=tables[part].at[me],
-            send_sem=lat_s.at[part, target], recv_sem=lat_r.at[part, me],
+            send_sem=lat_s.at[part], recv_sem=lat_r.at[part],
             device_id={"section": 1, "sp": target}, device_id_type=MESH,
         )
 
-    def latent_arrival(part, source):
-        rows = pl.ds(parts[part][0] // 2, parts[part][1] // 2)
-        return pltpu.make_async_remote_copy(
-            src_ref=lat_mine.at[rows], dst_ref=tables[part].at[source],
-            send_sem=lat_s.at[part, source], recv_sem=lat_r.at[part, source],
-            device_id={"section": 0, "sp": source}, device_id_type=MESH,
-        )
-
-    def drain(step, carry):
-        target = to_peer(step)
-        for c in (0, 1, 2):
-            qkv_copy(c, target).wait_send()
-        sibling_copy(target).wait_send()
-        return carry
-
-    lax.fori_loop(1, n_sp, drain, 0)
-    sibling_copy(me).wait_send()
-
-    def drain_branch(step, carry):
-        for part in range(len(parts)):
-            branch_copy(part, to_peer(step)).wait_send()
-        return carry
+    for c in (0, 1, 2):
+        all_sent(stage.at[c, pl.ds(0, 2 * (n_sp - 1))], s_sem.at[c])
+    all_sent(att_send, sib_s)
 
     wanted_copy = pltpu.make_async_copy(wanted_held, wanted_out, out_sem.at[1])
     brl_copy = pltpu.make_async_copy(brl, brl_out, out_sem.at[2])
@@ -430,11 +415,7 @@
     @pl.when(sec == 0)
     def _():
         for part, (start, size) in enumerate(parts):
-            def returned(step, carry, part=part):
-                branch_arrival(part, from_peer(step)).wait_recv()
-                return carry
-
-            lax.fori_loop(1, n_sp, returned, 0)
+            all_arrived(branches(brl, part), br_r.at[part])
             total = jnp.zeros((size, width), F32)
             for source in range(n_sp):
                 total = total + lax.dot_general(
@@ -457,34 +438,23 @@
         wanted_held[...] = jnp.zeros_like(wanted_held)
         wanted_copy.start()
         brl_copy.start()
-        lax.fori_loop(1, n_sp, drain_branch, 0)
         for part in range(len(parts)):
-            def handed(step, carry, part=part):
-                latent_copy(part, to_peer(step)).wait_send()
-                return carry
-
-            lax.fori_loop(0, n_sp, handed, 0)
+            all_sent(branches(brs, part), br_s.at[part])
+            all_sent(tables[part], lat_s.at[part])
             swap_copy(part).wait_send()
 
     @pl.when(sec == 1)
     def _():
         lanes = lax.broadcasted_iota(jnp.int32, (tok, 2 * width), 1)
 
-        def arrived(step, carry):
-            for part in range(len(parts)):
-                branch_arrival(part, from_peer(step)).wait_recv()
-            return carry
-
-        lax.fori_loop(1, n_sp, arrived, 0)
+        for part in range(len(parts)):
+            all_arrived(branches(brl, part), br_r.at[part])
         brl_copy.start()
-        lax.fori_loop(1, n_sp, drain_branch, 0)
+        for part in range(len(parts)):
+            all_sent(branches(brs, part), br_s.at[part])
         picked = jnp.zeros((tok, 2 * width), F32)
         for part, (onehot, table) in enumerate(zip(onehots, tables)):
-            def latent_in(step, carry, part=part):
-                latent_arrival(part, from_peer(step)).wait_recv()
-                return carry
-
-            lax.fori_loop(0, n_sp, latent_in, 0)
+            all_arrived(table, lat_r.at[part])
             rows = table[...].reshape(n_sp * parts[part][1] // 2, 2 * width)
             low = jnp.dot(onehot[0], rows, preferred_element_type=F32)
             high = jnp.dot(onehot[1], rows, preferred_element_type=F32)
@@ -565,11 +535,11 @@
             pltpu.SMEM((1, 1), jnp.int32),
             pltpu.VMEM((1, tok), jnp.int32),
             dma((3,)), dma((5,)), dma((3,)),
-            dma((3, n_sp)), dma((3, n_sp)),
-            dma((n_sp,)), dma((n_sp,)),
-            dma((3, n_sp)), dma((3, n_sp)),
+            dma((3,)), dma((3,)), dma((n_sp,)),
+            dma, dma((n_sp,)),
             dma((3,)), dma((3,)),
-            dma((3, n_sp)), dma((3, n_sp)),
+            dma((3,)), dma((3,)),
+            dma((3,)), dma((3,)),
             dma((2,)), dma((2,)), dma((3,)),
         ],
         compiler_params=pltpu.CompilerParams(

time: 125 us -> 122 us (0.976)
  Pallas kernels: 123 us -> 120 us
    pallas_call x1, Pallas kernels: 120 us -> 118 us  [on_device(): pl.pallas_call(body, name='guided_attention', out_shape=(jax.ShapeDtypeSt...]
where the time goes in v4:
time: 122 us; the launch traced here: 121 us
  Pallas kernels  120 us (98%)
  between operations  1.3 us (1%)
    pallas_call x1, Pallas kernels, on_device(): pl.pallas_call(body, name='guided_attention', out_shape=(jax.ShapeDtypeSt...  118 us

profile of v4, /device:TPU:20, one launch (start us, length us, event | category | flops | bytes accessed | tf_op | source)
XLA Modules:
  0.0 121.3 jit_solution(13418845073130205579)
XLA Ops:
  1.3 117.5 %guided_attention.1 = (bf16[16,160,128]{2,1,0:T(8,128)(2,1)}, bf16[160,128]{1,0:T(8,128)(2,1)}, bf16[128,2048]{1,0:T(8,128)(2,1)}) custom-call(bf16[160,3,32,128]{3,2,1,0:T(8,128)(2,1)} %bitcast.6, s32[1,1]{1,0:T(1,128)S(6)} %copy.8.refs_1_, s32[1,1]{1,0:T(1,128)S(6)} %copy.9.refs_2_, s32[1,160]{1,0:T(1,128)} %bitcast.8, bf16[32,64,128]{2,1,0:T(8,128)(2,1)} %bitcast.7, ...), custom_call_target="tpu_custom_call" | custom-call | tf_op jit(solution)/shard_map/guided_attention/pallas_call | solution.py:500
  118.9 2.4 %lift.1 = bf16[160,16,128]{2,1,0:T(8,128)(2,1)} custom-call(bf16[160,128]{1,0:T(8,128)(2,1)} %get-tuple-element.8.wanted_ref, bf16[128,2048]{1,0:T(8,128)(2,1)} %get-tuple-element.9.w2_ref, bf16[16,160,128]{2,1,0:T(8,128)(2,1)} %get-tuple-element.10.brl_ref), custom_call_target="tpu_custom_call" | custom-call | tf_op jit(solution)/shard_map/lift/pallas_call | solution.py:556

commit v5 on v4

--- a/solution.py
+++ b/solution.py
@@ -140,7 +140,7 @@
 
     def send_kind(c):
         def body(step, carry):
-            qkv_copy(c, to_peer(step)).start()
+            qkv_copy(c, to_peer(n_sp - step)).start()
             return carry
 
         lax.fori_loop(1, n_sp, body, 0)
@@ -189,9 +189,9 @@
 
     def send_most(c):
         def body(step, carry):
-            @pl.when(jnp.logical_or(sec == 1, step != across))
+            @pl.when(jnp.logical_or(sec == 1, n_sp - step != across))
             def _():
-                qkv_copy(c, to_peer(step)).start()
+                qkv_copy(c, to_peer(n_sp - step)).start()
 
             return carry
 

time: 122 us -> 122 us (level)
  no operation moved by 1% of the time
where the time goes in v5:
time: 122 us; the launch traced here: 120 us
  Pallas kernels  119 us (98%)
  between operations  1.3 us (1%)
    pallas_call x1, Pallas kernels, on_device(): pl.pallas_call(body, name='guided_attention', out_shape=(jax.ShapeDtypeSt...  116 us

profile of v5, /device:TPU:20, one launch (start us, length us, event | category | flops | bytes accessed | tf_op | source)
XLA Modules:
  0.0 120.2 jit_solution(17707548656270485715)
XLA Ops:
  1.3 116.5 %guided_attention.1 = (bf16[16,160,128]{2,1,0:T(8,128)(2,1)}, bf16[160,128]{1,0:T(8,128)(2,1)}, bf16[128,2048]{1,0:T(8,128)(2,1)}) custom-call(bf16[160,3,32,128]{3,2,1,0:T(8,128)(2,1)} %bitcast.6, s32[1,1]{1,0:T(1,128)S(6)} %copy.8.refs_1_, s32[1,1]{1,0:T(1,128)S(6)} %copy.9.refs_2_, s32[1,160]{1,0:T(1,128)} %bitcast.8, bf16[32,64,128]{2,1,0:T(8,128)(2,1)} %bitcast.7, ...), custom_call_target="tpu_custom_call" | custom-call | tf_op jit(solution)/shard_map/guided_attention/pallas_call | solution.py:500
  117.8 2.4 %lift.1 = bf16[160,16,128]{2,1,0:T(8,128)(2,1)} custom-call(bf16[160,128]{1,0:T(8,128)(2,1)} %get-tuple-element.8.wanted_ref, bf16[128,2048]{1,0:T(8,128)(2,1)} %get-tuple-element.9.w2_ref, bf16[16,160,128]{2,1,0:T(8,128)(2,1)} %get-tuple-element.10.brl_ref), custom_call_target="tpu_custom_call" | custom-call | tf_op jit(solution)/shard_map/lift/pallas_call | solution.py:556

commit v6 on v5

--- a/solution.py
+++ b/solution.py
@@ -430,7 +430,7 @@
             lat_mine[rows] = (packed + psum_recv[rows]).astype(BF16)
 
             def hand(step, carry, part=part):
-                latent_copy(part, to_peer(step)).start()
+                latent_copy(part, to_peer(n_sp - 1 - step)).start()
                 return carry
 
             lax.fori_loop(0, n_sp, hand, 0)

time: 122 us -> 121 us (level)
  no operation moved by 1% of the time
where the time goes in v6:
time: 121 us; the launch traced here: 120 us
  Pallas kernels  119 us (98%)
  between operations  1.3 us (1%)
    pallas_call x1, Pallas kernels, on_device(): pl.pallas_call(body, name='guided_attention', out_shape=(jax.ShapeDtypeSt...  116 us
    pallas_call x1, Pallas kernels, on_device(): pl.pallas_call(lift_kernel, name='lift', out_shape=jax.ShapeDtypeStruct((...  2.42 us

profile of v6, /device:TPU:20, one launch (start us, length us, event | category | flops | bytes accessed | tf_op | source)
XLA Modules:
  0.0 119.8 jit_solution(515550306109717898)
XLA Ops:
  1.3 116.1 %guided_attention.1 = (bf16[16,160,128]{2,1,0:T(8,128)(2,1)}, bf16[160,128]{1,0:T(8,128)(2,1)}, bf16[128,2048]{1,0:T(8,128)(2,1)}) custom-call(bf16[160,3,32,128]{3,2,1,0:T(8,128)(2,1)} %bitcast.6, s32[1,1]{1,0:T(1,128)S(6)} %copy.8.refs_1_, s32[1,1]{1,0:T(1,128)S(6)} %copy.9.refs_2_, s32[1,160]{1,0:T(1,128)} %bitcast.8, bf16[32,64,128]{2,1,0:T(8,128)(2,1)} %bitcast.7, ...), custom_call_target="tpu_custom_call" | custom-call | tf_op jit(solution)/shard_map/guided_attention/pallas_call | solution.py:500
  117.4 2.4 %lift.1 = bf16[160,16,128]{2,1,0:T(8,128)(2,1)} custom-call(bf16[160,128]{1,0:T(8,128)(2,1)} %get-tuple-element.8.wanted_ref, bf16[128,2048]{1,0:T(8,128)(2,1)} %get-tuple-element.9.w2_ref, bf16[16,160,128]{2,1,0:T(8,128)(2,1)} %get-tuple-element.10.brl_ref), custom_call_target="tpu_custom_call" | custom-call | tf_op jit(solution)/shard_map/lift/pallas_call | solution.py:556

commit v7 on v6

--- a/solution.py
+++ b/solution.py
@@ -384,7 +384,7 @@
 
     for part in range(1, len(parts)):
         def send_rest(step, carry, part=part):
-            send_part(part, step)
+            send_part(part, n_sp - step if part == len(parts) - 1 else step)
             return carry
 
         lax.fori_loop(1, n_sp, send_rest, 0)

time: 121 us -> 121 us (level)
  no operation moved by 1% of the time
where the time goes in v7:
time: 121 us; the launch traced here: 119 us
  Pallas kernels  118 us (98%)
  between operations  1.3 us (1%)
    pallas_call x1, Pallas kernels, on_device(): pl.pallas_call(body, name='guided_attention', out_shape=(jax.ShapeDtypeSt...  116 us
    pallas_call x1, Pallas kernels, on_device(): pl.pallas_call(lift_kernel, name='lift', out_shape=jax.ShapeDtypeStruct((...  2.42 us

profile of v7, /device:TPU:20, one launch (start us, length us, event | category | flops | bytes accessed | tf_op | source)
XLA Modules:
  0.0 119.4 jit_solution(4265148506230285556)
XLA Ops:
  1.3 115.7 %guided_attention.1 = (bf16[16,160,128]{2,1,0:T(8,128)(2,1)}, bf16[160,128]{1,0:T(8,128)(2,1)}, bf16[128,2048]{1,0:T(8,128)(2,1)}) custom-call(bf16[160,3,32,128]{3,2,1,0:T(8,128)(2,1)} %bitcast.6, s32[1,1]{1,0:T(1,128)S(6)} %copy.8.refs_1_, s32[1,1]{1,0:T(1,128)S(6)} %copy.9.refs_2_, s32[1,160]{1,0:T(1,128)} %bitcast.8, bf16[32,64,128]{2,1,0:T(8,128)(2,1)} %bitcast.7, ...), custom_call_target="tpu_custom_call" | custom-call | tf_op jit(solution)/shard_map/guided_attention/pallas_call | solution.py:500
  117.0 2.4 %lift.1 = bf16[160,16,128]{2,1,0:T(8,128)(2,1)} custom-call(bf16[160,128]{1,0:T(8,128)(2,1)} %get-tuple-element.8.wanted_ref, bf16[128,2048]{1,0:T(8,128)(2,1)} %get-tuple-element.9.w2_ref, bf16[16,160,128]{2,1,0:T(8,128)(2,1)} %get-tuple-element.10.brl_ref), custom_call_target="tpu_custom_call" | custom-call | tf_op jit(solution)/shard_map/lift/pallas_call | solution.py:556
